TPU v7x, 32 devices: a whole 2x2x4 slice. The times are simulated.
32 devices in a mesh: train: 8 (over z, y), dom: 4 (over x, core).
Axes of the slice: x: 2, y: 2, z: 4, core: 2. Of those that a mesh axis runs over, the one named last changes fastest.
Arguments:
- particles: float32 [4, 512, 4096], P(None, 'train', 'dom'), may hold values from -16 to 16
- slice_bin: int32 [512, 4096], P('train', 'dom'), may hold values from 0 to 127
- bunch_counts: int32 [512], P('train'), may hold values from 1365 to 4096, as said below
- past_moments: float32 [2, 512, 64], P(None, 'train'), may hold values from -6 to 6
- wake_lags: float32 [1535], replicated, may hold values from 0 to 2
- wake_matrix: float32 [64, 64], replicated, may hold values from -0.1875 to 0.1875
- adjust_phase: float32 [2], replicated, may hold values from -3.140625 to 3.140625
Outputs:
- tracked: float32 [4, 512, 4096], P(None, 'train', 'dom')
- moments_now: float32 [512, 64], P('train')
Inputs may be any that keep to these rules, and one draw needn't show every extreme that they name: `bunch_counts`: some bunch holds exactly 4096 live macroparticles in every draw.
All inputs are finite; a program needn't handle non-finite values.
Results may differ from a plain program's by a relative error of at most 0.0003.
Values sent between devices are 32-bit elements; how exact they have to be, the bound alone decides.
A program may use at most 64 MiB of HBM per device.

v0:
```python
import math

import jax
import jax.numpy as jnp
from jax import lax
from jax.sharding import PartitionSpec as P

NBIN = 128


def legendre_table(count_bins, orders):
    centers = 2.0 * (jnp.arange(count_bins, dtype=jnp.float32) + 0.5) / count_bins - 1.0
    columns = [jnp.ones_like(centers), centers]
    for degree in range(1, orders - 1):
        columns.append(
            ((2 * degree + 1) * centers * columns[degree] - degree * columns[degree - 1])
            / (degree + 1)
        )
    return jnp.stack(columns[:orders], axis=1)


def wake_response_kernel(targets, number, turn_back, bunches_all, wake_lags):
    sources = jnp.arange(number, dtype=jnp.int32)
    lag_index = targets[:, None] - sources[None, :] + turn_back * bunches_all
    table_index = jnp.clip(lag_index - 1, 0, wake_lags.shape[0] - 1)
    values = jnp.take(wake_lags, table_index)
    return jnp.where(lag_index > 0, values, jnp.zeros_like(values))


def exact_dot(left, right):
    return jnp.dot(left, right, precision=lax.Precision.HIGHEST, preferred_element_type=jnp.float32)


def local(particles, slice_bin, bunch_counts, past_moments, wake_lags, wake_matrix, adjust_phase):
    bunches = particles.shape[1]
    slot_width = particles.shape[2]
    orders = wake_matrix.shape[0] // 2
    bunch_sections = lax.axis_size("train")
    bunches_all = bunches * bunch_sections
    dom_index = lax.axis_index("dom")
    train_index = lax.axis_index("train")
    legendre_basis = legendre_table(NBIN, orders)
    slot_index = dom_index * slot_width + jnp.arange(slot_width, dtype=jnp.int32)
    alive_particle_mask = (slot_index[None, :] < bunch_counts[:, None]).astype(jnp.float32)
    planes = jnp.stack((particles[0], particles[2])) * alive_particle_mask[None]
    bin_values = jnp.arange(NBIN, dtype=jnp.int32)
    block_rows = math.gcd(bunches, 32)
    block_count = bunches // block_rows

    def histogram(block_index):
        bin_block = lax.dynamic_slice_in_dim(slice_bin, block_index * block_rows, block_rows, 0)
        value_block = lax.dynamic_slice_in_dim(planes, block_index * block_rows, block_rows, 1)
        one_hot = (bin_block[:, :, None] == bin_values).astype(jnp.float32)
        return jnp.einsum("cbw,bwn->bcn", value_block, one_hot, precision=lax.Precision.HIGHEST)

    slice_binned = lax.map(histogram, jnp.arange(block_count, dtype=jnp.int32)).reshape(
        bunches, 2, NBIN
    )
    degree_weight = (2 * jnp.arange(orders, dtype=jnp.int32) + 1).astype(jnp.float32)
    projected_moments = jnp.einsum(
        "bcn,nk->bck", slice_binned, legendre_basis, precision=lax.Precision.HIGHEST
    )
    partial_terms = (
        projected_moments
        * degree_weight[None, None, :]
        / bunch_counts.astype(jnp.float32)[:, None, None]
    ).reshape(bunches, 2 * orders)
    local_bunch_first = train_index * bunches
    targets = local_bunch_first + jnp.arange(bunches, dtype=jnp.int32)
    moments_now = lax.psum(partial_terms, "dom")
    pieces = (
        lax.all_gather(past_moments[0], "train", axis=0, tiled=True),
        lax.all_gather(past_moments[1], "train", axis=0, tiled=True),
    )
    count_here = pieces[0].shape[0]
    older = exact_dot(
        wake_response_kernel(targets, count_here, 1, bunches_all, wake_lags), pieces[0]
    )
    oldest = exact_dot(
        wake_response_kernel(targets, count_here, 2, bunches_all, wake_lags), pieces[1]
    )
    convolved = older + oldest
    shard_piece = lax.all_gather(moments_now, "train", axis=0, tiled=True)
    kernel = wake_response_kernel(targets, shard_piece.shape[0], 0, bunches_all, wake_lags)
    convolved = convolved + exact_dot(kernel, shard_piece)
    kick_modes = exact_dot(convolved, wake_matrix)
    kick_table = jnp.einsum(
        "bck,nk->bcn",
        kick_modes.reshape(bunches, 2, orders),
        legendre_basis,
        precision=lax.Precision.HIGHEST,
    )

    def lookup(block_index):
        bin_block = lax.dynamic_slice_in_dim(slice_bin, block_index * block_rows, block_rows, 0)
        table_block = lax.dynamic_slice_in_dim(kick_table, block_index * block_rows, block_rows, 0)
        one_hot = (bin_block[:, :, None] == bin_values).astype(jnp.float32)
        return jnp.einsum("bwn,bcn->cbw", one_hot, table_block, precision=lax.Precision.HIGHEST)

    kick_field = lax.map(lookup, jnp.arange(block_count, dtype=jnp.int32))
    kick_field = kick_field.transpose(1, 0, 2, 3).reshape(2, bunches, slot_width)
    cosine = jnp.cos(adjust_phase)
    sine_phase = jnp.sin(adjust_phase)
    tracked = jnp.stack(
        (
            cosine[0] * particles[0] + sine_phase[0] * particles[1],
            -sine_phase[0] * particles[0] + cosine[0] * particles[1] + kick_field[0],
            cosine[1] * particles[2] + sine_phase[1] * particles[3],
            -sine_phase[1] * particles[2] + cosine[1] * particles[3] + kick_field[1],
        )
    )
    return (tracked, moments_now)


def solution(mesh):
    in_specs = (
        P(None, "train", "dom"),
        P("train", "dom"),
        P("train"),
        P(None, "train", None),
        P(),
        P(),
        P(),
    )
    out_specs = (P(None, "train", "dom"), P("train", None))
    return jax.shard_map(local, mesh=mesh, in_specs=in_specs, out_specs=out_specs, check_vma=False)
```

profile of v0, /device:TPU:0, one launch (start us, length us, event | category | flops | bytes accessed | tf_op | source)
XLA Modules:
  0.0 709.0 jit_solution(3386607870717800086)
XLA Ops:
  0.6 0.0 copy-start
  0.7 0.7 convert_element_type.21
  1.3 0.0 copy-start.1
  1.4 0.7 fusion.88
  2.1 0.7 fusion.86
  4.3 0.1 broadcast_multiply_fusion.15
  4.3 0.1 broadcast_multiply_fusion.13
  4.4 0.1 broadcast_multiply_fusion.11
  4.4 0.1 broadcast_multiply_fusion.9
  4.5 0.1 broadcast_multiply_fusion.7
  4.6 0.1 multiply_add_fusion.2
  4.7 0.1 subtract_multiply_fusion
  4.8 0.1 stack.7
  4.9 0.8 fusion.85
  5.7 32.5 %all-gather.1 = f32[1,512,64]{2,1,0:T(8,128)S(1)} all-gather(f32[1,64,64]{2,1,0:T(8,128)S(1)} %get-tuple-element.149), channel_id=3, replica_groups=mesh['train'=8,'dom'=4] {'train'}, dimensions={1}, use_global_device_ids=true | all-gather | bytes 147456 | tf_op jit(solution)/shard_map/all_gather | solution.py:73
  38.2 0.7 compare_convert_fusion
  39.0 30.7 %all-gather = f32[1,512,64]{2,1,0:T(8,128)S(1)} all-gather(f32[1,64,64]{2,1,0:T(8,128)S(1)} %get-tuple-element.150), channel_id=2, replica_groups=mesh['train'=8,'dom'=4] {'train'}, dimensions={1}, use_global_device_ids=true | all-gather | bytes 147456 | tf_op jit(solution)/shard_map/all_gather | solution.py:72
  69.7 0.2 fusion.25
  70.0 0.0 copy-done.1
  70.0 180.5 %gather_fusion.2 = f32[32768]{0:T(1024)S(1)} fusion(f32[1535]{0:T(1024)S(1)} %copy-done.1, s32[32768]{0:T(1024)S(1)} %broadcast_clamp_fusion), kind=kCustom, calls=%fused_computation.2.clone | custom fusion | bytes 393216 | tf_op jit(solution)/shard_map/jit(_take)/gather | solution.py:26
  250.6 180.5 %gather_fusion = f32[32768]{0:T(1024)S(1)} fusion(f32[1535]{0:T(1024)S(1)} %copy-done.1, s32[32768]{0:T(1024)S(1)} %broadcast_clamp_fusion.2), kind=kCustom, calls=%fused_computation.clone | custom fusion | bytes 393216 | tf_op jit(solution)/shard_map/jit(_take)/gather | solution.py:26
  431.2 0.4 fusion.16
  431.7 0.0 copy-start.3
  431.7 180.5 %gather_fusion.1 = f32[32768]{0:T(1024)S(1)} fusion(f32[1535]{0:T(1024)S(1)} %copy-done.1, s32[32768]{0:T(1024)S(1)} %broadcast_clamp_fusion.1), kind=kCustom, calls=%fused_computation.1.clone | custom fusion | bytes 393216 | tf_op jit(solution)/shard_map/jit(_take)/gather | solution.py:26
  612.3 0.4 convolution_add_fusion.1
  612.7 0.0 copy-done.3
  612.7 0.0 copy-start.2
  612.8 0.1 maximum_multiply_fusion
  612.8 0.8 copy-done.2
  613.6 22.1 %while.22 = (s32[]{:T(128)}, f32[2,32,2,128]{3,2,1,0:T(2,128)S(1)}, s32[2]{0:T(128)S(1)}, f32[2,64,1024]{2,1,0:T(8,128)S(1)}, s32[64,1024]{1,0:T(8,128)S(1)}, /*...) while((s32[]{:T(128)}, f32[2,32,2,128]{3,2,1,0:T(2,128)S(1)}, s32[2]{0:T(128)S(1)}, ...), condition=%wide.region_1.3_spmd.clone, body=%wide.region_0.2_spmd.clone.sunk | while | flops 104857608 | bytes 1212587 | solution.py:56
  613.6 0.6 dynamic_slice.37
  614.9 9.7 %fusion.99 = f32[2,32,2,128]{3,2,1,0:T(2,128)S(1)} fusion(f32[2,32,2,128]{3,2,1,0:T(2,128)S(1)} %get-tuple-element.262, s32[]{:T(128)S(6)} %copy.41, s32[32,1024]{1,0:T(8,128)S(1)} %constant_dynamic-slice_fusion.8, f32[2,32,1024]{2,1,0:T(8,128)S(1)} %constant_dynamic-slice_fusion.9), kind=kOutput, calls=%fused_computation.9.clone.1 | convolution fusion | flops 104857600 | bytes 425988 | tf_op jit(solution)/shard_map/while/body/eval_jaxpr/cbw,bwn->bcn/dot_general | solution.py:54
  624.7 0.6 dynamic_slice.37
  626.0 9.7 %fusion.99 = f32[2,32,2,128]{3,2,1,0:T(2,128)S(1)} fusion(f32[2,32,2,128]{3,2,1,0:T(2,128)S(1)} %get-tuple-element.262, s32[]{:T(128)S(6)} %copy.41, s32[32,1024]{1,0:T(8,128)S(1)} %constant_dynamic-slice_fusion.8, f32[2,32,1024]{2,1,0:T(8,128)S(1)} %constant_dynamic-slice_fusion.9), kind=kOutput, calls=%fused_computation.9.clone.1 | convolution fusion | flops 104857600 | bytes 425988 | tf_op jit(solution)/shard_map/while/body/eval_jaxpr/cbw,bwn->bcn/dot_general | solution.py:54
  635.7 0.3 fusion.14
  636.0 0.1 copy.16
  636.1 10.3 %psum.7 = f32[64,64]{1,0:T(8,128)S(1)} all-reduce(f32[64,64]{1,0:T(8,128)S(1)} %copy.16), channel_id=1, replica_groups=mesh['train'=8,'dom'=4] {'dom'}, use_global_device_ids=true, to_apply=%region_2.4 | all-reduce | flops 4096 | bytes 32768 | tf_op jit(solution)/shard_map/psum | solution.py:70
  646.4 0.0 copy-start.4
  646.4 30.9 %all_gather.11 = f32[512,64]{1,0:T(8,128)S(1)} all-gather(f32[64,64]{1,0:T(8,128)S(1)} %psum.7), channel_id=1, replica_groups=mesh['train'=8,'dom'=4] {'train'}, dimensions={0}, use_global_device_ids=true | all-gather | bytes 147456 | tf_op jit(solution)/shard_map/all_gather | solution.py:83
  677.3 0.4 convolution_add_fusion
  677.7 0.0 copy-done
  677.7 0.2 fusion.89
  677.9 0.3 fusion.59
  678.2 0.0 copy-done.4
  678.2 26.4 %while.23 = (s32[]{:T(128)}, f32[2,2,32,1024]{3,1,2,0:T(2,128)S(1)}, s32[2]{0:T(128)S(1)}, f32[64,2,128]{2,0,1:T(8,128)S(1)}, s32[64,1024]{1,0:T(8,128)S(1)}, /*...) while((s32[]{:T(128)}, f32[2,2,32,1024]{3,1,2,0:T(2,128)S(1)}, s32[2]{0:T(128)S(1)}, ...), condition=%wide.region_4.6_spmd.clone, body=%wide.region_3.5_spmd.clone.sunk | while | flops 104857608 | bytes 753835 | solution.py:100
  678.3 0.6 dynamic_slice.40
  679.5 11.9 %fusion.101 = f32[2,2,32,1024]{3,1,2,0:T(2,128)S(1)} fusion(f32[2,2,32,1024]{3,1,2,0:T(2,128)S(1)} %get-tuple-element.289, s32[]{:T(128)S(6)} %copy.47, s32[32,1024]{1,0:T(8,128)S(1)} %constant_dynamic-slice_fusion.10, f32[32,2,128]{2,0,1:T(8,128)S(1)} %constant_dynamic-slice_fusion.11), kind=kOutput, calls=%fused_computation.17.clone.1 | convolution fusion | flops 104857600 | bytes 425988 | tf_op jit(solution)/shard_map/while/body/eval_jaxpr/bwn,bcn->cbw/dot_general | solution.py:98
  691.4 0.6 dynamic_slice.40
  692.7 11.9 %fusion.101 = f32[2,2,32,1024]{3,1,2,0:T(2,128)S(1)} fusion(f32[2,2,32,1024]{3,1,2,0:T(2,128)S(1)} %get-tuple-element.289, s32[]{:T(128)S(6)} %copy.47, s32[32,1024]{1,0:T(8,128)S(1)} %constant_dynamic-slice_fusion.10, f32[32,2,128]{2,0,1:T(8,128)S(1)} %constant_dynamic-slice_fusion.11), kind=kOutput, calls=%fused_computation.17.clone.1 | convolution fusion | flops 104857600 | bytes 425988 | tf_op jit(solution)/shard_map/while/body/eval_jaxpr/bwn,bcn->cbw/dot_general | solution.py:98
  704.6 0.4 fusion.84
  705.1 2.8 multiply_add_fusion.1
  707.9 1.0 pad_maximum_fusion
  (37 shorter events, 0.7 us)
Async XLA Ops:
  0.6 677.0 %copy-start = (f32[64,64]{1,0:T(8,128)S(1)}, f32[64,64]{1,0:T(8,128)}, u32[]{:S(2)}) copy-start(f32[64,64]{1,0:T(8,128)} %param.18) | copy-start | bytes 49156
  1.3 68.6 %copy-start.1 = (f32[1535]{0:T(1024)S(1)}, f32[1535]{0:T(1024)}, u32[]{:S(2)}) copy-start(f32[1535]{0:T(1024)} %param.17) | copy-start | bytes 18424
  431.7 181.0 %copy-start.3 = (f32[4,64,1024]{2,1,0:T(8,128)S(1)}, f32[4,64,1024]{2,1,0:T(8,128)}, u32[]{:S(2)}) copy-start(f32[4,64,1024]{2,1,0:T(8,128)} %param.13) | copy-start | bytes 3145732
  612.7 1.0 copy-start.2
  646.4 31.9 %copy-start.4 = (f32[64,64]{1,0:T(8,128)}, f32[64,64]{1,0:T(8,128)S(1)}, u32[]{:S(2)}) copy-start(f32[64,64]{1,0:T(8,128)S(1)} %psum.7) | copy-start | bytes 49156
where the time goes:
time: 709 us
  local copies, waits for them, and re-layouts  548 us (77%)
  blocking collectives  104 us (15%)
  matrix products  45.2 us (6%)
    gather x6, local copies, waits for them, and re-layouts, wake_response_kernel(): values = jnp.take(wake_lags, table_index)  542 us
    all_gather x1, blocking collectives, local(): lax.all_gather(past_moments[1], 'train', axis=0, tiled=True)  32.5 us
    all_gather x1, blocking collectives, local(): shard_piece = lax.all_gather(moments_now, 'train', axis=0, tiled=True)  30.9 us
    all_gather x1, blocking collectives, local(): lax.all_gather(past_moments[0], 'train', axis=0, tiled=True)  30.7 us
    dot_general x2, matrix products, lookup(): jnp.einsum('bwn,bcn->cbw', one_hot, table_block, precision=lax.Precision....  23.8 us
    dot_general x2, matrix products, histogram(): jnp.einsum('cbw,bwn->bcn', value_block, one_hot, precision=lax.Precision....  19.4 us

commit v1 on v0

v1 whole, which is shorter than its diff:
```python
import functools

import jax
import jax.numpy as jnp
import numpy as np
from jax import lax
from jax.experimental import pallas as pl
from jax.experimental.pallas import tpu as pltpu
from jax.sharding import PartitionSpec as P

NBIN = 128
LANES = 128
MESH = pl.DeviceIdType.MESH
F32 = jnp.float32
BF16 = jnp.bfloat16


def split(a):
    high = a.astype(BF16)
    return high, (a - high.astype(F32)).astype(BF16)


def dot(a, b):
    return jnp.dot(a, b, preferred_element_type=F32)


def dot3(a_parts, b_parts):
    (ah, al), (bh, bl) = a_parts, b_parts
    return dot(ah, bh) + (dot(ah, bl) + dot(al, bh))


def lane_iota(rows):
    return lax.broadcasted_iota(jnp.int32, (rows, LANES), 1)


def merge(a, b, distance):
    low = (lane_iota(a.shape[0]) & distance) == 0
    return jnp.where(low, a, b) + pltpu.roll(jnp.where(low, b, a), distance, 1)


def tile_sum(a):
    parts = [a[:, i : i + LANES] for i in range(0, a.shape[1], LANES)]
    while len(parts) > 1:
        parts = [p + q for p, q in zip(parts[::2], parts[1::2])] + parts[len(parts) & ~1 :]
    return parts[0]


def moments_kernel(
    sections, doms, orders,
    particles, bins, counts, past, lags, wake, phase,
    table_out, coef_out, moments_out,
    x_buf, y_buf, bin_buf, e_buf, basis_buf, count_buf,
    mine, now_buf, past_buf, dom_buf, conv_mine, conv_buf,
    load_sem, past_send, past_recv, now_send, now_recv, dom_send, dom_recv, conv_send, conv_recv,
):
    bunches = counts.shape[1]
    half = bunches // 2
    chunks = half // 8
    width = 2 * orders
    bunches_all = bunches * sections
    own = 2 * sections // doms
    t = lax.axis_index("train")
    d = lax.axis_index("dom")

    barrier = pltpu.get_barrier_semaphore()
    for o in range(1, sections):
        pl.semaphore_signal(
            barrier, inc=1, device_id=(lax.rem(t + o, sections), d), device_id_type=MESH
        )
    for o in range(1, doms):
        pl.semaphore_signal(
            barrier, inc=1, device_id=(t, lax.rem(d + o, doms)), device_id_type=MESH
        )
    loads = [
        pltpu.make_async_copy(particles.at[0], x_buf, load_sem.at[0]),
        pltpu.make_async_copy(particles.at[2], y_buf, load_sem.at[1]),
        pltpu.make_async_copy(bins, bin_buf, load_sem.at[2]),
    ]
    for copy in loads:
        copy.start()

    angle = phase[...]
    cosine, sine = jnp.cos(angle), jnp.sin(angle)
    for plane in range(2):
        coef_out[2 * plane : 2 * plane + 1, :] = jnp.broadcast_to(
            cosine[:, plane : plane + 1], (1, LANES)
        )
        coef_out[2 * plane + 1 : 2 * plane + 2, :] = jnp.broadcast_to(
            sine[:, plane : plane + 1], (1, LANES)
        )
    eye = lax.broadcasted_iota(jnp.int32, (bunches, bunches), 0) == lax.broadcasted_iota(
        jnp.int32, (bunches, bunches), 1
    )
    count_f = counts[...].astype(F32)
    column = jnp.sum(jnp.where(eye, count_f, 0.0), axis=1, keepdims=True)
    count_buf[...] = jnp.broadcast_to(column, (bunches, LANES))

    basis_buf[...] = jnp.zeros_like(basis_buf)
    centers = (lane_iota(1).astype(F32) + 0.5) * (2.0 / NBIN) - 1.0
    previous, current = jnp.ones_like(centers), centers
    for k in range(orders):
        basis_buf[k : k + 1, 0:LANES] = previous
        basis_buf[orders + k : orders + k + 1, LANES : 2 * LANES] = previous
        following = ((2 * k + 3) * centers * current - (k + 1) * previous) / (k + 2)
        previous, current = current, following
    to_kick = dot3(split(wake[...]), split(basis_buf[...]))
    to_kick = jnp.concatenate([to_kick, to_kick], axis=0)
    to_kick = split(to_kick)

    rows = bunches_all // 32
    pad = e_buf.shape[0] - rows
    count_lags = lags.shape[1]
    e_buf[...] = jnp.zeros_like(e_buf)
    for row in range(pl.cdiv(count_lags, LANES)):
        size = min(LANES, count_lags - row * LANES)
        e_buf[pad + row : pad + row + 1, 0:size] = lags[:, row * LANES : row * LANES + size]
    plain = e_buf[...]
    lane = lane_iota(plain.shape[0])
    turned = jnp.take_along_axis(plain, LANES - 1 - lane, axis=1, mode="promise_in_bounds")
    moved = pltpu.roll(turned, LANES // 2, 1)
    mixed = jnp.where(lane < LANES // 2, moved, pltpu.roll(moved, 1, 0))
    odd = lax.rem(t, 2)
    e_buf[...] = jnp.where(odd == 1, mixed, turned)
    first_row = pad + rows - 1 - bunches_all // 64 + (t + 1) // 2
    target = lax.broadcasted_iota(jnp.int32, (bunches, LANES), 0)
    source = lane_iota(bunches)

    def toeplitz(tile_first, tiles):
        def rolled(m):
            row = e_buf[pl.ds(first_row - m, 1), :]
            return pltpu.roll(
                jnp.broadcast_to(row, (bunches, LANES)), 0, 1, stride=1, stride_axis=0
            )

        turned_rows = [rolled(tile_first + m) for m in range(-1, tiles)]
        return jnp.concatenate(
            [
                jnp.where(source >= target, turned_rows[m + 1], turned_rows[m])
                for m in range(tiles)
            ],
            axis=1,
        )

    w_now = split(toeplitz(2 * bunches_all // LANES, bunches_all // LANES))
    past_tiles = own * bunches // LANES
    w_past = split(toeplitz(d * past_tiles, past_tiles))

    pl.semaphore_wait(barrier, sections - 1 + doms - 1)
    late = t // own == d
    owned = jnp.logical_or(late, (sections + t) // own == d)
    turn = jnp.where(late, 1, 0)
    slot = lax.rem(t, own)

    def past_copy(o):
        return pltpu.make_async_remote_copy(
            src_ref=past.at[turn], dst_ref=past_buf.at[slot],
            send_sem=past_send.at[o - 1], recv_sem=past_recv.at[slot],
            device_id=(lax.rem(t + o, sections), d), device_id_type=MESH,
        )

    @pl.when(owned)
    def _():
        for o in range(1, sections):
            past_copy(o).start()
        past_buf[slot] = past[turn]

    for copy in loads:
        copy.wait()
    slots = x_buf.shape[1]
    slot_index = d * slots + lax.broadcasted_iota(jnp.int32, (8, slots), 1)
    k_lane = lane_iota(8) % orders
    scale = jnp.ones((8, LANES), F32)
    lead = 1.0
    for k in range(1, orders):
        lead = lead * (2 * k - 1) / k
        scale = jnp.where(k_lane == k, np.float32((2 * k + 1) * lead), scale)
    low_half = lane_iota(8) < width

    def group_sums(first):
        here = pl.ds(first, 8)
        z = (bin_buf[here, :].astype(F32) + 0.5) * (2.0 / NBIN) - 1.0
        count = count_buf[here, 0:1].astype(jnp.int32)
        alive = slot_index < count
        vx = jnp.where(alive, x_buf[here, :], 0.0)
        vy = jnp.where(alive, y_buf[here, :], 0.0)
        stacks = ([], [])
        before, at = None, None
        for k in range(orders):
            if k == 0:
                terms = (vx, vy)
            else:
                if k == 1:
                    before, at = jnp.ones_like(z), z
                elif k == 2:
                    before, at = at, z * at - np.float32(1 / 3)
                else:
                    n = k - 1
                    before, at = at, z * at - np.float32(n * n / (4 * n * n - 1)) * before
                terms = (vx * at, vy * at)
            for stack, term in zip(stacks, terms):
                value, level = tile_sum(term), 1
                while stack and stack[-1][1] == level:
                    value = merge(stack.pop()[0], value, level)
                    level *= 2
                stack.append((value, level))
        return merge(stacks[0][0][0], stacks[1][0][0], orders)

    def now_copy(o, j):
        return pltpu.make_async_remote_copy(
            src_ref=mine.at[j], dst_ref=now_buf.at[t, j],
            send_sem=now_send.at[o - 1, j], recv_sem=now_recv.at[o - 1, j],
            device_id=(lax.rem(t + o, sections), d), device_id_type=MESH,
        )

    def dom_copy(o, j):
        return pltpu.make_async_remote_copy(
            src_ref=mine.at[j], dst_ref=dom_buf.at[d, j],
            send_sem=dom_send.at[o - 1, j], recv_sem=dom_recv.at[o - 1, j],
            device_id=(t, lax.rem(d + o, doms)), device_id_type=MESH,
        )

    def chunk(j, carry):
        first = pl.multiple_of(j * 8, 8)
        second = pl.multiple_of(j * 8 + half, 8)
        total = merge(group_sums(first), group_sums(second), width)
        divisor = jnp.where(
            low_half, count_buf[pl.ds(first, 8), :], count_buf[pl.ds(second, 8), :]
        )
        moments = total * scale / divisor
        mine[j] = moments
        for o in range(1, sections):
            now_copy(o, j).start()
        for o in range(1, doms):
            dom_copy(o, j).start()
        now_buf[t, j] = moments
        dom_buf[d, j] = moments
        return carry

    lax.fori_loop(0, chunks, chunk, 0)

    for s in range(own):
        @pl.when(lax.rem(d * own + s, sections) != t)
        def _():
            pltpu.make_async_remote_copy(
                src_ref=past.at[0], dst_ref=past_buf.at[s],
                send_sem=past_send.at[0], recv_sem=past_recv.at[s],
                device_id=(t, d), device_id_type=MESH,
            ).wait_recv()
    stored = past_buf[...].reshape(own * bunches, width)
    convolved = dot3(w_past, split(stored))

    for o in range(1, sections):
        for j in range(chunks):
            now_copy(o, j).wait_recv()
    gathered = now_buf[...].reshape(sections, half, LANES)
    lower = lane_iota(half)[None] < width
    spread = jnp.concatenate(
        [jnp.where(lower, gathered, 0.0), jnp.where(lower, 0.0, gathered)], axis=1
    ).reshape(bunches_all, LANES)
    both = dot3(w_now, split(spread))
    convolved = convolved + (both[:, :width] + both[:, width:])
    packed = jnp.concatenate([convolved[:half], convolved[half:]], axis=1)
    conv_mine[...] = packed

    def conv_copy(o):
        return pltpu.make_async_remote_copy(
            src_ref=conv_mine, dst_ref=conv_buf.at[d],
            send_sem=conv_send.at[o - 1], recv_sem=conv_recv.at[o - 1],
            device_id=(t, lax.rem(d + o, doms)), device_id_type=MESH,
        )

    for o in range(1, doms):
        conv_copy(o).start()
    conv_buf[d] = packed

    for o in range(1, doms):
        for j in range(chunks):
            dom_copy(o, j).wait_recv()
    summed = dom_buf[0]
    for i in range(1, doms):
        summed = summed + dom_buf[i]
    summed = summed.reshape(half, LANES)
    moments_out[0:half, :] = summed[:, :width]
    moments_out[half:bunches, :] = summed[:, width:]

    for o in range(1, doms):
        conv_copy(o).wait_recv()
    total = conv_buf[0]
    for i in range(1, doms):
        total = total + conv_buf[i]
    lower = lane_iota(half) < width
    total = jnp.concatenate([jnp.where(lower, total, 0.0), jnp.where(lower, 0.0, total)], axis=0)
    table_out[...] = dot3(split(total), to_kick)

    @pl.when(owned)
    def _():
        for o in range(1, sections):
            past_copy(o).wait_send()

    for o in range(1, sections):
        for j in range(chunks):
            now_copy(o, j).wait_send()
    for o in range(1, doms):
        for j in range(chunks):
            dom_copy(o, j).wait_send()
        conv_copy(o).wait_send()


def track_kernel(particles, bins, table, coef, moments, tracked, moments_out):
    rows, slots = bins.shape
    for plane in range(2):
        cosine = jnp.broadcast_to(coef[2 * plane : 2 * plane + 1, :], (rows, LANES))
        sine = jnp.broadcast_to(coef[2 * plane + 1 : 2 * plane + 2, :], (rows, LANES))
        kicks = table[:, plane * NBIN : (plane + 1) * NBIN]
        for first in range(0, slots, LANES):
            here = slice(first, first + LANES)
            place, momentum = particles[2 * plane, :, here], particles[2 * plane + 1, :, here]
            kick = jnp.take_along_axis(kicks, bins[:, here], axis=1, mode="promise_in_bounds")
            tracked[2 * plane, :, here] = cosine * place + sine * momentum
            tracked[2 * plane + 1, :, here] = cosine * momentum - sine * place + kick
    moments_out[...] = moments[...]


def local(sections, doms, particles, slice_bin, bunch_counts, past_moments, wake_lags, wake_matrix, adjust_phase):
    _, bunches, slots = particles.shape
    width = wake_matrix.shape[0]
    orders = width // 2
    half = bunches // 2
    chunks = half // 8
    bunches_all = bunches * sections
    own = 2 * sections // doms
    lag_rows = bunches_all // 32
    pad = pl.cdiv(bunches_all // 128, 8) * 8
    vmem = pl.BlockSpec(memory_space=pltpu.VMEM)
    hbm = pl.BlockSpec(memory_space=pl.ANY)
    dma = pltpu.SemaphoreType.DMA
    table, coef, moments = pl.pallas_call(
        functools.partial(moments_kernel, sections, doms, orders),
        out_shape=(
            jax.ShapeDtypeStruct((bunches, 2 * NBIN), F32),
            jax.ShapeDtypeStruct((4, LANES), F32),
            jax.ShapeDtypeStruct((bunches, width), F32),
        ),
        in_specs=[hbm, hbm, vmem, vmem, vmem, vmem, vmem],
        out_specs=(vmem, vmem, vmem),
        scratch_shapes=[
            pltpu.VMEM((bunches, slots), F32),
            pltpu.VMEM((bunches, slots), F32),
            pltpu.VMEM((bunches, slots), jnp.int32),
            pltpu.VMEM((pad + lag_rows, LANES), F32),
            pltpu.VMEM((width, 2 * NBIN), F32),
            pltpu.VMEM((bunches, LANES), F32),
            pltpu.VMEM((chunks, 8, LANES), F32),
            pltpu.VMEM((sections, chunks, 8, LANES), F32),
            pltpu.VMEM((own, bunches, width), F32),
            pltpu.VMEM((doms, chunks, 8, LANES), F32),
            pltpu.VMEM((half, LANES), F32),
            pltpu.VMEM((doms, half, LANES), F32),
            dma((3,)),
            dma((sections - 1,)),
            dma((own,)),
            dma((sections - 1, chunks)),
            dma((sections - 1, chunks)),
            dma((doms - 1, chunks)),
            dma((doms - 1, chunks)),
            dma((doms - 1,)),
            dma((doms - 1,)),
        ],
        compiler_params=pltpu.CompilerParams(
            collective_id=0, has_side_effects=True, vmem_limit_bytes=32 * 1024 * 1024
        ),
        name="moments",
    )(
        particles,
        slice_bin,
        bunch_counts.reshape(1, -1),
        past_moments,
        wake_lags.reshape(1, -1),
        wake_matrix,
        adjust_phase.reshape(1, -1),
    )
    block = 16
    return pl.pallas_call(
        track_kernel,
        grid=(bunches // block,),
        out_shape=(
            jax.ShapeDtypeStruct(particles.shape, F32),
            jax.ShapeDtypeStruct((bunches, width), F32),
        ),
        in_specs=[
            pl.BlockSpec((4, block, slots), lambda i: (0, i, 0)),
            pl.BlockSpec((block, slots), lambda i: (i, 0)),
            pl.BlockSpec((block, 2 * NBIN), lambda i: (i, 0)),
            pl.BlockSpec((4, LANES), lambda i: (0, 0)),
            pl.BlockSpec((bunches, width), lambda i: (0, 0)),
        ],
        out_specs=(
            pl.BlockSpec((4, block, slots), lambda i: (0, i, 0)),
            pl.BlockSpec((bunches, width), lambda i: (0, 0)),
        ),
        compiler_params=pltpu.CompilerParams(vmem_limit_bytes=32 * 1024 * 1024),
        name="track",
    )(particles, slice_bin, table, coef, moments)


def solution(mesh):
    in_specs = (
        P(None, "train", "dom"),
        P("train", "dom"),
        P("train"),
        P(None, "train", None),
        P(),
        P(),
        P(),
    )
    out_specs = (P(None, "train", "dom"), P("train", None))
    body = functools.partial(local, mesh.shape["train"], mesh.shape["dom"])
    return jax.shard_map(body, mesh=mesh, in_specs=in_specs, out_specs=out_specs, check_vma=False)
```

time: 709 us -> 24.7 us (0.03)
  local copies, waits for them, and re-layouts: 548 us -> 4.49 us
  blocking collectives: 104 us -> 0 us
  matrix products: 45.2 us -> 0 us
  Pallas kernels: 0 us -> 19.2 us
    gather x6 -> x0, local copies, waits for them, and re-layouts: 542 us -> none  [wake_response_kernel(): values = jnp.take(wake_lags, table_index)]
    all_gather x3 -> x0, blocking collectives: 94.2 us -> none  [the longest x1 32.5 us: local(): lax.all_gather(past_moments[1], 'train', axis=0, tiled=True)]
    dot_general x10 -> x0, matrix products: 45.2 us -> none  [the longest x2 23.8 us: lookup(): jnp.einsum('bwn,bcn->cbw', one_hot, table_block, precision=lax.Precision....]
    pallas_call x0 -> x2, Pallas kernels: none -> 19.2 us  [the longest x1 17.2 us: local(): pl.pallas_call(functools.partial(moments_kernel, sections, doms, orders),...]
    psum x1 -> x0, blocking collectives: 10.3 us -> none  [local(): moments_now = lax.psum(partial_terms, 'dom')]
where the time goes in v1:
time: 24.7 us; the launch traced here: 24.3 us
  Pallas kernels  19.2 us (78%)
  local copies, waits for them, and re-layouts  4.49 us (18%)
  between operations  0.67 us (3%)
    pallas_call x1, Pallas kernels, local(): pl.pallas_call(functools.partial(moments_kernel, sections, doms, orders),...  17.2 us
    unnamed x12, local copies, waits for them, and re-layouts  3.77 us
    pallas_call x1, Pallas kernels, local(): pl.pallas_call(track_kernel, grid=(bunches // block,), out_shape=(jax.Sha...  1.98 us
    reshape x1, local copies, waits for them, and re-layouts, local(): wake_lags.reshape(1, -1)  0.71 us

profile of v1, /device:TPU:0, one launch (start us, length us, event | category | flops | bytes accessed | tf_op | source)
XLA Modules:
  0.0 24.3 jit_solution(15109591776350171468)
XLA Ops:
  0.6 0.0 copy-start.4
  0.6 0.0 copy-start.5
  0.7 0.7 %reshape.14.lags = f32[1,1535]{1,0:T(1,128)S(1)} reshape(f32[1535]{0:T(1024)} %param.11) | data formatting | bytes 12280 | tf_op jit(solution)/shard_map/reshape | solution.py:378
  1.4 0.0 copy-done.4
  1.4 0.0 copy-done.5
  1.4 0.0 copy-start
  1.4 1.2 %copy-done = f32[4,64,1024]{2,1,0:T(8,128)S(1)} copy-done((f32[4,64,1024]{2,1,0:T(8,128)S(1)}, f32[4,64,1024]{2,1,0:T(8,128)}, u32[]{:S(2)}) %copy-start) | copy-done | bytes 1048600
  2.6 0.0 copy-start.1
  2.6 0.9 %copy-done.1 = s32[64,1024]{1,0:T(8,128)S(1)} copy-done((s32[64,1024]{1,0:T(8,128)S(1)}, s32[64,1024]{1,0:T(8,128)}, u32[]{:S(2)}) %copy-start.1) | copy-done | bytes 262168
  3.6 0.0 copy-start.2
  3.6 0.8 %copy-done.2 = f32[2,64,64]{2,1,0:T(8,128)S(1)} copy-done((f32[2,64,64]{2,1,0:T(8,128)S(1)}, f32[2,64,64]{2,1,0:T(8,128)}, u32[]{:S(2)}) %copy-start.2) | copy-done | bytes 32792
  4.4 0.0 copy-start.3
  4.4 0.8 %copy-done.3 = f32[64,64]{1,0:T(8,128)S(1)} copy-done((f32[64,64]{1,0:T(8,128)S(1)}, f32[64,64]{1,0:T(8,128)}, u32[]{:S(2)}) %copy-start.3) | copy-done | bytes 16408
  5.1 17.2 %moments.1 = (f32[64,256]{1,0:T(8,128)S(1)}, f32[4,128]{1,0:T(4,128)S(1)}, f32[64,64]{1,0:T(8,128)S(1)}) custom-call(f32[4,64,1024]{2,1,0:T(8,128)S(1)} %copy-done, s32[64,1024]{1,0:T(8,128)S(1)} %copy-done.1, s32[1,64]{1,0:T(1,128)S(1)} %bitcast.2, f32[2,64,64]{2,1,0:T(8,128)S(1)} %copy-done.2, f32[1,1535]{1,0:T(1,128)S(1)} %reshape.14.lags, ...), custom_call_target="tpu_custom_call" | custom-call | tf_op jit(solution)/shard_map/moments/pallas_call | solution.py:337
  22.4 2.0 %track.1 = (f32[4,64,1024]{2,1,0:T(8,128)}, f32[64,64]{1,0:T(8,128)}) custom-call(f32[4,64,1024]{2,1,0:T(8,128)S(1)} %copy-done, s32[64,1024]{1,0:T(8,128)S(1)} %copy-done.1, f32[64,256]{1,0:T(8,128)S(1)} %get-tuple-element.5.table, f32[4,128]{1,0:T(4,128)S(1)} %get-tuple-element.6.coef, f32[64,64]{1,0:T(8,128)S(1)} %get-tuple-element.7.moments), custom_call_target="tpu_custom_call" | custom-call | tf_op jit(solution)/shard_map/track/pallas_call | solution.py:383
Async XLA Ops:
  0.6 0.7 %copy-start.4 = (s32[64]{0:T(128)S(1)}, s32[64]{0:T(128)}, u32[]{:S(2)}) copy-start(s32[64]{0:T(128)} %param.9) | copy-start | bytes 772
  0.6 0.7 %copy-start.5 = (f32[2]{0:T(128)S(1)}, f32[2]{0:T(128)}, u32[]{:S(2)}) copy-start(f32[2]{0:T(128)} %param.13) | copy-start | bytes 28
  1.4 1.2 %copy-start = (f32[4,64,1024]{2,1,0:T(8,128)S(1)}, f32[4,64,1024]{2,1,0:T(8,128)}, u32[]{:S(2)}) copy-start(f32[4,64,1024]{2,1,0:T(8,128)} %particles.3) | copy-start | bytes 3145732
  2.6 0.9 %copy-start.1 = (s32[64,1024]{1,0:T(8,128)S(1)}, s32[64,1024]{1,0:T(8,128)}, u32[]{:S(2)}) copy-start(s32[64,1024]{1,0:T(8,128)} %bins.3) | copy-start | bytes 786436
  3.6 0.8 %copy-start.2 = (f32[2,64,64]{2,1,0:T(8,128)S(1)}, f32[2,64,64]{2,1,0:T(8,128)}, u32[]{:S(2)}) copy-start(f32[2,64,64]{2,1,0:T(8,128)} %past.1) | copy-start | bytes 98308
  4.4 0.8 %copy-start.3 = (f32[64,64]{1,0:T(8,128)S(1)}, f32[64,64]{1,0:T(8,128)}, u32[]{:S(2)}) copy-start(f32[64,64]{1,0:T(8,128)} %wake.1) | copy-start | bytes 49156

commit v2 on v1

v2 whole, which is shorter than its diff:
```python
import functools

import jax
import jax.numpy as jnp
import numpy as np
from jax import lax
from jax.experimental import pallas as pl
from jax.experimental.pallas import tpu as pltpu
from jax.sharding import PartitionSpec as P

NBIN = 128
LANES = 128
MESH = pl.DeviceIdType.MESH
F32 = jnp.float32
BF16 = jnp.bfloat16


def split(a):
    high = a.astype(BF16)
    return high, (a - high.astype(F32)).astype(BF16)


def dot(a, b):
    return jnp.dot(a, b, preferred_element_type=F32)


def dot3(a_parts, b_parts):
    (ah, al), (bh, bl) = a_parts, b_parts
    return dot(ah, bh) + (dot(ah, bl) + dot(al, bh))


def lane_iota(rows):
    return lax.broadcasted_iota(jnp.int32, (rows, LANES), 1)


def merge(a, b, distance):
    low = (lane_iota(a.shape[0]) & distance) == 0
    return jnp.where(low, a, b) + pltpu.roll(jnp.where(low, b, a), distance, 1)


def tile_sum(a):
    parts = [a[:, i : i + LANES] for i in range(0, a.shape[1], LANES)]
    while len(parts) > 1:
        parts = [p + q for p, q in zip(parts[::2], parts[1::2])] + parts[len(parts) & ~1 :]
    return parts[0]


def moments_kernel(
    sections, doms, orders,
    particles, bins, counts, past, lags, wake, phase,
    out,
    x_buf, y_buf, bin_buf, count_in, lag_in, wake_in, phase_in, e_buf, basis_buf, count_buf,
    now_buf, past_buf, dom_buf, conv_buf,
    load_sem, past_send, past_recv, pair_sem,
):
    bunches = counts.shape[1]
    half = bunches // 2
    chunks = half // 8
    width = 2 * orders
    bunches_all = bunches * sections
    own = 2 * sections // doms
    t = lax.axis_index("train")
    d = lax.axis_index("dom")
    now_send, now_recv, dom_send, dom_recv, conv_send, conv_recv = [pair_sem.at[i] for i in range(6)]

    barrier = pltpu.get_barrier_semaphore()
    for o in range(1, sections):
        pl.semaphore_signal(
            barrier, inc=1, device_id=(lax.rem(t + o, sections), d), device_id_type=MESH
        )
    for o in range(1, doms):
        pl.semaphore_signal(
            barrier, inc=1, device_id=(t, lax.rem(d + o, doms)), device_id_type=MESH
        )
    pairs = [
        (counts, count_in),
        (bins, bin_buf),
        (particles.at[0], x_buf),
        (particles.at[2], y_buf),
        (lags, lag_in),
        (wake, wake_in),
        (phase, phase_in),
    ]
    loads = [
        pltpu.make_async_copy(src, dst, load_sem.at[i]) for i, (src, dst) in enumerate(pairs)
    ]
    for copy in loads:
        copy.start()

    late = t // own == d
    owned = jnp.logical_or(late, (sections + t) // own == d)
    turn = jnp.where(late, 1, 0)
    slot = lax.rem(t, own)

    def past_copy(o):
        return pltpu.make_async_remote_copy(
            src_ref=past.at[turn], dst_ref=past_buf.at[slot],
            send_sem=past_send.at[o - 1], recv_sem=past_recv.at[slot],
            device_id=(lax.rem(t + o, sections), d), device_id_type=MESH,
        )

    def past_here():
        return pltpu.make_async_copy(past.at[turn], past_buf.at[slot], load_sem.at[len(pairs)])

    @pl.when(owned)
    def _():
        past_here().start()

    basis_buf[...] = jnp.zeros_like(basis_buf)
    centers = (lane_iota(1).astype(F32) + 0.5) * (2.0 / NBIN) - 1.0
    previous, current = jnp.ones_like(centers), centers
    for k in range(orders):
        basis_buf[k : k + 1, 0:LANES] = previous
        basis_buf[orders + k : orders + k + 1, LANES : 2 * LANES] = previous
        following = np.float32((2 * k + 3) / (k + 2)) * centers * current
        following = following - np.float32((k + 1) / (k + 2)) * previous
        previous, current = current, following

    loads[0].wait()
    eye = lax.broadcasted_iota(jnp.int32, (bunches, bunches), 0) == lax.broadcasted_iota(
        jnp.int32, (bunches, bunches), 1
    )
    count_f = count_in[...].astype(F32)
    column = jnp.sum(jnp.where(eye, count_f, 0.0), axis=1, keepdims=True)
    count_buf[...] = jnp.broadcast_to(column, (bunches, LANES))

    pl.semaphore_wait(barrier, sections - 1 + doms - 1)

    @pl.when(owned)
    def _():
        for o in range(1, sections):
            past_copy(o).start()

    for copy in loads[1:4]:
        copy.wait()
    slots = x_buf.shape[1]
    slot_index = d * slots + lax.broadcasted_iota(jnp.int32, (8, slots), 1)
    k_lane = lane_iota(8) % orders
    scale = jnp.ones((8, LANES), F32)
    lead = 1.0
    for k in range(1, orders):
        lead = lead * (2 * k - 1) / k
        scale = jnp.where(k_lane == k, np.float32((2 * k + 1) * lead), scale)
    low_half = lane_iota(8) < width

    def group_sums(first):
        here = pl.ds(first, 8)
        z = (bin_buf[here, :].astype(F32) + 0.5) * (2.0 / NBIN) - 1.0
        count = count_buf[here, 0:1].astype(jnp.int32)
        alive = slot_index < count
        vx = jnp.where(alive, x_buf[here, :], 0.0)
        vy = jnp.where(alive, y_buf[here, :], 0.0)
        stacks = ([], [])
        before, at = None, None
        for k in range(orders):
            if k == 0:
                terms = (vx, vy)
            else:
                if k == 1:
                    before, at = jnp.ones_like(z), z
                elif k == 2:
                    before, at = at, z * at - np.float32(1 / 3)
                else:
                    n = k - 1
                    before, at = at, z * at - np.float32(n * n / (4 * n * n - 1)) * before
                terms = (vx * at, vy * at)
            for stack, term in zip(stacks, terms):
                value, level = tile_sum(term), 1
                while stack and stack[-1][1] == level:
                    value = merge(stack.pop()[0], value, level)
                    level *= 2
                stack.append((value, level))
        return merge(stacks[0][0][0], stacks[1][0][0], orders)

    def chunk(j, carry):
        first = pl.multiple_of(j * 8, 8)
        second = pl.multiple_of(j * 8 + half, 8)
        total = merge(group_sums(first), group_sums(second), width)
        divisor = jnp.where(
            low_half, count_buf[pl.ds(first, 8), :], count_buf[pl.ds(second, 8), :]
        )
        moments = total * scale / divisor
        now_buf[t, j] = moments
        dom_buf[d, j] = moments
        for o in range(1, sections):
            pltpu.make_async_remote_copy(
                src_ref=now_buf.at[t, j], dst_ref=now_buf.at[t, j],
                send_sem=now_send, recv_sem=now_recv,
                device_id=(lax.rem(t + o, sections), d), device_id_type=MESH,
            ).start()
        return carry

    lax.fori_loop(0, chunks, chunk, 0)

    def dom_copies(ref, send_sem, recv_sem):
        for o in range(1, doms):
            pltpu.make_async_remote_copy(
                src_ref=ref.at[d], dst_ref=ref.at[d], send_sem=send_sem, recv_sem=recv_sem,
                device_id=(t, lax.rem(d + o, doms)), device_id_type=MESH,
            ).start()

    def whole(ref, send_sem, recv_sem):
        part = ref.at[pl.ds(0, ref.shape[0] - 1)]
        return pltpu.make_async_remote_copy(
            src_ref=part, dst_ref=part, send_sem=send_sem, recv_sem=recv_sem,
            device_id=(t, d), device_id_type=MESH,
        )

    dom_copies(dom_buf, dom_send, dom_recv)

    loads[4].wait()
    rows = bunches_all // 32
    pad = e_buf.shape[0] - rows
    count_lags = lag_in.shape[-1]
    e_buf[...] = jnp.zeros_like(e_buf)
    for row in range(pl.cdiv(count_lags, LANES)):
        size = min(LANES, count_lags - row * LANES)
        e_buf[pad + row : pad + row + 1, 0:size] = lag_in[pl.ds(row * LANES, size)].reshape(1, size)
    plain = e_buf[...]
    lane = lane_iota(plain.shape[0])
    turned = jnp.take_along_axis(plain, LANES - 1 - lane, axis=1, mode="promise_in_bounds")
    moved = pltpu.roll(turned, LANES // 2, 1)
    mixed = jnp.where(lane < LANES // 2, moved, pltpu.roll(moved, 1, 0))
    odd = lax.rem(t, 2)
    e_buf[...] = jnp.where(odd == 1, mixed, turned)
    first_row = pad + rows - 1 - bunches_all // 64 + (t + 1) // 2
    target = lax.broadcasted_iota(jnp.int32, (bunches, LANES), 0)
    source = lane_iota(bunches)

    def toeplitz(tile_first, tiles):
        def rolled(m):
            row = e_buf[pl.ds(first_row - m, 1), :]
            return pltpu.roll(
                jnp.broadcast_to(row, (bunches, LANES)), 0, 1, stride=1, stride_axis=0
            )

        turned_rows = [rolled(tile_first + m) for m in range(-1, tiles)]
        return jnp.concatenate(
            [
                jnp.where(source >= target, turned_rows[m + 1], turned_rows[m])
                for m in range(tiles)
            ],
            axis=1,
        )

    w_now = split(toeplitz(2 * bunches_all // LANES, bunches_all // LANES))
    past_tiles = own * bunches // LANES
    w_past = split(toeplitz(d * past_tiles, past_tiles))

    for s in range(own):
        @pl.when(lax.rem(d * own + s, sections) != t)
        def _():
            pltpu.make_async_remote_copy(
                src_ref=past.at[0], dst_ref=past_buf.at[s],
                send_sem=past_send.at[0], recv_sem=past_recv.at[s],
                device_id=(t, d), device_id_type=MESH,
            ).wait_recv()

    @pl.when(owned)
    def _():
        past_here().wait()

    stored = past_buf[...].reshape(own * bunches, width)
    convolved = dot3(w_past, split(stored))

    whole(now_buf, now_send, now_recv).wait_recv()
    gathered = now_buf[...].reshape(sections, half, LANES)
    lower = lane_iota(half)[None] < width
    spread = jnp.concatenate(
        [jnp.where(lower, gathered, 0.0), jnp.where(lower, 0.0, gathered)], axis=1
    ).reshape(bunches_all, LANES)
    both = dot3(w_now, split(spread))
    convolved = convolved + (both[:, :width] + both[:, width:])
    conv_buf[d] = jnp.concatenate([convolved[:half], convolved[half:]], axis=1)
    dom_copies(conv_buf, conv_send, conv_recv)

    for copy in loads[5:]:
        copy.wait()
    to_kick = dot3(split(wake_in[...]), split(basis_buf[...]))
    to_kick = jnp.concatenate([to_kick, to_kick], axis=0)
    to_kick = split(to_kick)
    angle = phase_in[...]
    cosine, sine = jnp.cos(angle), jnp.sin(angle)
    for plane in range(2):
        row = 2 * bunches + 2 * plane
        out[row : row + 1, :] = jnp.broadcast_to(cosine[:, plane : plane + 1], (1, 2 * NBIN))
        out[row + 1 : row + 2, :] = jnp.broadcast_to(sine[:, plane : plane + 1], (1, 2 * NBIN))
    dom_wait = whole(dom_buf, dom_send, dom_recv)
    dom_wait.wait_recv()
    summed = dom_buf[0]
    for i in range(1, doms):
        summed = summed + dom_buf[i]
    summed = summed.reshape(half, LANES)
    out[bunches : bunches + half, 0:width] = summed[:, :width]
    out[bunches + half : 2 * bunches, 0:width] = summed[:, width:]

    @pl.when(owned)
    def _():
        for o in range(1, sections):
            past_copy(o).wait_send()

    whole(now_buf, now_send, now_recv).wait_send()
    dom_wait.wait_send()

    conv_wait = whole(conv_buf, conv_send, conv_recv)
    conv_wait.wait_recv()
    total = conv_buf[0]
    for i in range(1, doms):
        total = total + conv_buf[i]
    lower = lane_iota(half) < width
    total = jnp.concatenate([jnp.where(lower, total, 0.0), jnp.where(lower, 0.0, total)], axis=0)
    out[0:bunches, :] = dot3(split(total), to_kick)
    conv_wait.wait_send()


def track_kernel(particles, bins, table, tracked, moments_out, result, moments, sems):
    bunches, slots = bins.shape
    block = 16
    moments[...] = table[bunches : 2 * bunches, 0 : moments.shape[1]]
    through = pltpu.make_async_copy(moments, moments_out, sems.at[bunches // block])
    through.start()
    copies = []
    for i in range(bunches // block):
        rows = slice(i * block, (i + 1) * block)
        for plane in range(2):
            row = 2 * bunches + 2 * plane
            cosine = jnp.broadcast_to(table[row : row + 1, 0:LANES], (block, LANES))
            sine = jnp.broadcast_to(table[row + 1 : row + 2, 0:LANES], (block, LANES))
            kicks = table[rows, plane * NBIN : (plane + 1) * NBIN]
            for first in range(0, slots, LANES):
                here = slice(first, first + LANES)
                place = particles[2 * plane, rows, here]
                momentum = particles[2 * plane + 1, rows, here]
                kick = jnp.take_along_axis(
                    kicks, bins[rows, here], axis=1, mode="promise_in_bounds"
                )
                result[2 * plane, rows, here] = cosine * place + sine * momentum
                result[2 * plane + 1, rows, here] = cosine * momentum - sine * place + kick
        copy = pltpu.make_async_copy(result.at[:, rows, :], tracked.at[:, rows, :], sems.at[i])
        copy.start()
        copies.append(copy)
    for copy in copies:
        copy.wait()
    through.wait()


def local(sections, doms, particles, slice_bin, bunch_counts, past_moments, wake_lags, wake_matrix, adjust_phase):
    _, bunches, slots = particles.shape
    width = wake_matrix.shape[0]
    orders = width // 2
    half = bunches // 2
    chunks = half // 8
    bunches_all = bunches * sections
    own = 2 * sections // doms
    lag_rows = bunches_all // 32
    pad = pl.cdiv(bunches_all // 128, 8) * 8
    vmem = pl.BlockSpec(memory_space=pltpu.VMEM)
    hbm = pl.BlockSpec(memory_space=pltpu.HBM)
    dma = pltpu.SemaphoreType.DMA
    table = pl.pallas_call(
        functools.partial(moments_kernel, sections, doms, orders),
        out_shape=jax.ShapeDtypeStruct((2 * bunches + 8, 2 * NBIN), F32),
        in_specs=[hbm] * 7,
        out_specs=vmem,
        scratch_shapes=[
            pltpu.VMEM((bunches, slots), F32),
            pltpu.VMEM((bunches, slots), F32),
            pltpu.VMEM((bunches, slots), jnp.int32),
            pltpu.VMEM((1, bunches), jnp.int32),
            pltpu.VMEM(wake_lags.shape, F32),
            pltpu.VMEM((width, width), F32),
            pltpu.VMEM((1, 2), F32),
            pltpu.VMEM((pad + lag_rows, LANES), F32),
            pltpu.VMEM((width, 2 * NBIN), F32),
            pltpu.VMEM((bunches, LANES), F32),
            pltpu.VMEM((sections, chunks, 8, LANES), F32),
            pltpu.VMEM((own, bunches, width), F32),
            pltpu.VMEM((doms, chunks, 8, LANES), F32),
            pltpu.VMEM((doms, half, LANES), F32),
            dma((8,)),
            dma((sections - 1,)),
            dma((own,)),
            dma((6,)),
        ],
        compiler_params=pltpu.CompilerParams(
            collective_id=0, has_side_effects=True, vmem_limit_bytes=56 * 1024 * 1024
        ),
        name="moments",
    )(
        particles,
        slice_bin,
        bunch_counts.reshape(1, -1),
        past_moments,
        wake_lags,
        wake_matrix,
        adjust_phase.reshape(1, -1),
    )
    return pl.pallas_call(
        track_kernel,
        out_shape=(
            jax.ShapeDtypeStruct(particles.shape, F32),
            jax.ShapeDtypeStruct((bunches, width), F32),
        ),
        in_specs=[vmem, vmem, vmem],
        out_specs=(hbm, hbm),
        scratch_shapes=[pltpu.VMEM(particles.shape, F32), pltpu.VMEM((bunches, width), F32), dma((bunches // 16 + 1,))],
        compiler_params=pltpu.CompilerParams(vmem_limit_bytes=16 * 1024 * 1024),
        name="track",
    )(particles, slice_bin, table)


def solution(mesh):
    in_specs = (
        P(None, "train", "dom"),
        P("train", "dom"),
        P("train"),
        P(None, "train", None),
        P(),
        P(),
        P(),
    )
    out_specs = (P(None, "train", "dom"), P("train", None))
    body = functools.partial(local, mesh.shape["train"], mesh.shape["dom"])
    return jax.shard_map(body, mesh=mesh, in_specs=in_specs, out_specs=out_specs, check_vma=False)
```

time: 24.7 us -> 20.5 us (0.83)
  local copies, waits for them, and re-layouts: 4.49 us -> 0.91 us
  Pallas kernels: 19.2 us -> 18.8 us
    unnamed x12 -> x6, local copies, waits for them, and re-layouts: 3.77 us -> 0.91 us
    pallas_call x1, Pallas kernels: 1.98 us -> 1.17 us  [local(): pl.pallas_call(track_kernel, out_shape=(jax.ShapeDtypeStruct(particles.sh...]
    reshape x1 -> x0, local copies, waits for them, and re-layouts: 0.71 us -> none  [local(): wake_lags.reshape(1, -1)]
    pallas_call x1, Pallas kernels: 17.2 us -> 17.6 us  [local(): pl.pallas_call(functools.partial(moments_kernel, sections, doms, orders),...]
where the time goes in v2:
time: 20.5 us; the launch traced here: 20.4 us
  Pallas kernels  18.8 us (92%)
  local copies, waits for them, and re-layouts  0.91 us (4%)
  between operations  0.68 us (3%)
    pallas_call x1, Pallas kernels, local(): pl.pallas_call(functools.partial(moments_kernel, sections, doms, orders),...  17.6 us
    pallas_call x1, Pallas kernels, local(): pl.pallas_call(track_kernel, out_shape=(jax.ShapeDtypeStruct(particles.sh...  1.17 us
    unnamed x6, local copies, waits for them, and re-layouts  0.91 us

profile of v2, /device:TPU:0, one launch (start us, length us, event | category | flops | bytes accessed | tf_op | source)
XLA Modules:
  0.0 20.4 jit_solution(6550294830275554740)
XLA Ops:
  0.6 0.0 copy-start
  0.6 0.0 copy-start.1
  0.7 17.6 %moments.1.table = f32[136,256]{1,0:T(8,128)} custom-call(f32[4,64,1024]{2,1,0:T(8,128)} %particles.3, s32[64,1024]{1,0:T(8,128)} %bins.3, s32[1,64]{1,0:T(1,128)} %bitcast.2, f32[2,64,64]{2,1,0:T(8,128)} %past.1, f32[1535]{0:T(1024)} %lags.1, f32[64,64]{1,0:T(8,128)} %wake.1, f32[1,2]{1,0:T(1,128)} %bitcast.3), custom_call_target="tpu_custom_call" | custom-call | tf_op jit(solution)/shard_map/moments/pallas_call | solution.py:360
  18.3 0.0 copy-done
  18.3 0.0 copy-done.1
  18.3 0.0 copy-start.2
  18.3 0.9 %copy-done.2 = f32[136,256]{1,0:T(8,128)S(1)} copy-done((f32[136,256]{1,0:T(8,128)S(1)}, f32[136,256]{1,0:T(8,128)}, u32[]{:S(2)}) %copy-start.2) | copy-done | bytes 139288
  19.2 1.2 %track.1 = (f32[4,64,1024]{2,1,0:T(8,128)}, f32[64,64]{1,0:T(8,128)}) custom-call(f32[4,64,1024]{2,1,0:T(8,128)S(1)} %copy-done, s32[64,1024]{1,0:T(8,128)S(1)} %copy-done.1, f32[136,256]{1,0:T(8,128)S(1)} %copy-done.2), custom_call_target="tpu_custom_call" | custom-call | tf_op jit(solution)/shard_map/track/pallas_call | solution.py:398
Async XLA Ops:
  0.6 17.6 %copy-start = (f32[4,64,1024]{2,1,0:T(8,128)S(1)}, f32[4,64,1024]{2,1,0:T(8,128)}, u32[]{:S(2)}) copy-start(f32[4,64,1024]{2,1,0:T(8,128)} %particles.3) | copy-start | bytes 3145732
  0.6 17.6 %copy-start.1 = (s32[64,1024]{1,0:T(8,128)S(1)}, s32[64,1024]{1,0:T(8,128)}, u32[]{:S(2)}) copy-start(s32[64,1024]{1,0:T(8,128)} %bins.3) | copy-start | bytes 786436
  18.3 0.9 %copy-start.2 = (f32[136,256]{1,0:T(8,128)S(1)}, f32[136,256]{1,0:T(8,128)}, u32[]{:S(2)}) copy-start(f32[136,256]{1,0:T(8,128)} %moments.1.table) | copy-start | bytes 417796

commit v3 on v2

--- a/solution.py
+++ b/solution.py
@@ -137,32 +137,31 @@
     slot_index = d * slots + lax.broadcasted_iota(jnp.int32, (8, slots), 1)
     k_lane = lane_iota(8) % orders
     scale = jnp.ones((8, LANES), F32)
-    lead = 1.0
     for k in range(1, orders):
-        lead = lead * (2 * k - 1) / k
-        scale = jnp.where(k_lane == k, np.float32((2 * k + 1) * lead), scale)
+        scale = jnp.where(k_lane == k, np.float32(2 * k + 1), scale)
     low_half = lane_iota(8) < width
 
     def group_sums(first):
         here = pl.ds(first, 8)
-        z = (bin_buf[here, :].astype(F32) + 0.5) * (2.0 / NBIN) - 1.0
+        places = bin_buf[here, :]
+        places = [places[:, i : i + LANES] for i in range(0, slots, LANES)]
         count = count_buf[here, 0:1].astype(jnp.int32)
         alive = slot_index < count
         vx = jnp.where(alive, x_buf[here, :], 0.0)
         vy = jnp.where(alive, y_buf[here, :], 0.0)
         stacks = ([], [])
-        before, at = None, None
         for k in range(orders):
             if k == 0:
                 terms = (vx, vy)
             else:
-                if k == 1:
-                    before, at = jnp.ones_like(z), z
-                elif k == 2:
-                    before, at = at, z * at - np.float32(1 / 3)
-                else:
-                    n = k - 1
-                    before, at = at, z * at - np.float32(n * n / (4 * n * n - 1)) * before
+                row = jnp.broadcast_to(basis_buf[k : k + 1, 0:LANES], (8, LANES))
+                at = jnp.concatenate(
+                    [
+                        jnp.take_along_axis(row, place, axis=1, mode="promise_in_bounds")
+                        for place in places
+                    ],
+                    axis=1,
+                )
                 terms = (vx * at, vy * at)
             for stack, term in zip(stacks, terms):
                 value, level = tile_sum(term), 1

time: 20.5 us -> 37.4 us (1.82)
  Pallas kernels: 18.8 us -> 35.6 us
    pallas_call x1, Pallas kernels: 17.6 us -> 34.4 us  [local(): pl.pallas_call(functools.partial(moments_kernel, sections, doms, orders),...]
where the time goes in v3:
time: 37.4 us; the launch traced here: 37.2 us
  Pallas kernels  35.6 us (95%)
  local copies, waits for them, and re-layouts  0.91 us (2%)
  between operations  0.68 us (2%)
    pallas_call x1, Pallas kernels, local(): pl.pallas_call(functools.partial(moments_kernel, sections, doms, orders),...  34.4 us
    pallas_call x1, Pallas kernels, local(): pl.pallas_call(track_kernel, out_shape=(jax.ShapeDtypeStruct(particles.sh...  1.17 us
    unnamed x6, local copies, waits for them, and re-layouts  0.91 us

profile of v3, /device:TPU:0, one launch (start us, length us, event | category | flops | bytes accessed | tf_op | source)
XLA Modules:
  0.0 37.2 jit_solution(12401593939486913575)
XLA Ops:
  0.6 0.0 copy-start
  0.6 0.0 copy-start.1
  0.7 34.4 %moments.1.table = f32[136,256]{1,0:T(8,128)} custom-call(f32[4,64,1024]{2,1,0:T(8,128)} %particles.3, s32[64,1024]{1,0:T(8,128)} %bins.3, s32[1,64]{1,0:T(1,128)} %bitcast.2, f32[2,64,64]{2,1,0:T(8,128)} %past.1, f32[1535]{0:T(1024)} %lags.1, f32[64,64]{1,0:T(8,128)} %wake.1, f32[1,2]{1,0:T(1,128)} %bitcast.3), custom_call_target="tpu_custom_call" | custom-call | tf_op jit(solution)/shard_map/moments/pallas_call | solution.py:359
  35.1 0.0 copy-done
  35.1 0.0 copy-done.1
  35.1 0.0 copy-start.2
  35.1 0.9 %copy-done.2 = f32[136,256]{1,0:T(8,128)S(1)} copy-done((f32[136,256]{1,0:T(8,128)S(1)}, f32[136,256]{1,0:T(8,128)}, u32[]{:S(2)}) %copy-start.2) | copy-done | bytes 139288
  36.0 1.2 %track.1 = (f32[4,64,1024]{2,1,0:T(8,128)}, f32[64,64]{1,0:T(8,128)}) custom-call(f32[4,64,1024]{2,1,0:T(8,128)S(1)} %copy-done, s32[64,1024]{1,0:T(8,128)S(1)} %copy-done.1, f32[136,256]{1,0:T(8,128)S(1)} %copy-done.2), custom_call_target="tpu_custom_call" | custom-call | tf_op jit(solution)/shard_map/track/pallas_call | solution.py:397
Async XLA Ops:
  0.6 34.5 %copy-start = (f32[4,64,1024]{2,1,0:T(8,128)S(1)}, f32[4,64,1024]{2,1,0:T(8,128)}, u32[]{:S(2)}) copy-start(f32[4,64,1024]{2,1,0:T(8,128)} %particles.3) | copy-start | bytes 3145732
  0.6 34.5 %copy-start.1 = (s32[64,1024]{1,0:T(8,128)S(1)}, s32[64,1024]{1,0:T(8,128)}, u32[]{:S(2)}) copy-start(s32[64,1024]{1,0:T(8,128)} %bins.3) | copy-start | bytes 786436
  35.1 0.9 %copy-start.2 = (f32[136,256]{1,0:T(8,128)S(1)}, f32[136,256]{1,0:T(8,128)}, u32[]{:S(2)}) copy-start(f32[136,256]{1,0:T(8,128)} %moments.1.table) | copy-start | bytes 417796

commit v4 on v3

--- a/solution.py
+++ b/solution.py
@@ -38,6 +38,29 @@
     return jnp.where(low, a, b) + pltpu.roll(jnp.where(low, b, a), distance, 1)
 
 
+def product_basis(orders):
+    nodes = np.cos((np.arange(orders) + 0.5) * np.pi / orders)
+    angle = np.arccos(nodes)
+    outer = orders // 8
+    products = np.stack(
+        [np.cos(8 * a * angle) * np.cos(j * angle) for j in range(8) for a in range(outer)], 1
+    )
+    legendre = np.polynomial.legendre.legvander(nodes, orders - 1)
+    return np.linalg.solve(products, legendre) * (2 * np.arange(orders) + 1)
+
+
+def plane_maps(orders):
+    outer = orders // 8
+    one = product_basis(orders)
+    both = np.zeros((2 * orders, 2 * orders))
+    for c in range(2):
+        for j in range(8):
+            for a in range(outer):
+                both[(j * 2 + c) * outer + a, c * orders : (c + 1) * orders] = one[j * outer + a]
+    twice = np.kron(np.eye(2), both)
+    return [m.astype(np.float32) for m in (both, np.linalg.inv(both), twice)]
+
+
 def tile_sum(a):
     parts = [a[:, i : i + LANES] for i in range(0, a.shape[1], LANES)]
     while len(parts) > 1:
@@ -47,9 +70,9 @@
 
 def moments_kernel(
     sections, doms, orders,
-    particles, bins, counts, past, lags, wake, phase,
+    particles, bins, counts, past, lags, wake, phase, to_moments, to_raw, to_both,
     out,
-    x_buf, y_buf, bin_buf, count_in, lag_in, wake_in, phase_in, e_buf, basis_buf, count_buf,
+    x_buf, y_buf, bin_buf, count_in, lag_in, wake_in, phase_in, to_moments_in, to_raw_in, to_both_in, e_buf, basis_buf, count_buf,
     now_buf, past_buf, dom_buf, conv_buf,
     load_sem, past_send, past_recv, pair_sem,
 ):
@@ -80,6 +103,9 @@
         (lags, lag_in),
         (wake, wake_in),
         (phase, phase_in),
+        (to_moments, to_moments_in),
+        (to_raw, to_raw_in),
+        (to_both, to_both_in),
     ]
     loads = [
         pltpu.make_async_copy(src, dst, load_sem.at[i]) for i, (src, dst) in enumerate(pairs)
@@ -135,41 +161,43 @@
         copy.wait()
     slots = x_buf.shape[1]
     slot_index = d * slots + lax.broadcasted_iota(jnp.int32, (8, slots), 1)
-    k_lane = lane_iota(8) % orders
-    scale = jnp.ones((8, LANES), F32)
-    for k in range(1, orders):
-        scale = jnp.where(k_lane == k, np.float32(2 * k + 1), scale)
     low_half = lane_iota(8) < width
+
+    outer = orders // 8
 
     def group_sums(first):
         here = pl.ds(first, 8)
-        places = bin_buf[here, :]
-        places = [places[:, i : i + LANES] for i in range(0, slots, LANES)]
         count = count_buf[here, 0:1].astype(jnp.int32)
-        alive = slot_index < count
-        vx = jnp.where(alive, x_buf[here, :], 0.0)
-        vy = jnp.where(alive, y_buf[here, :], 0.0)
-        stacks = ([], [])
-        for k in range(orders):
-            if k == 0:
-                terms = (vx, vy)
-            else:
-                row = jnp.broadcast_to(basis_buf[k : k + 1, 0:LANES], (8, LANES))
-                at = jnp.concatenate(
-                    [
-                        jnp.take_along_axis(row, place, axis=1, mode="promise_in_bounds")
-                        for place in places
-                    ],
-                    axis=1,
-                )
-                terms = (vx * at, vy * at)
-            for stack, term in zip(stacks, terms):
-                value, level = tile_sum(term), 1
-                while stack and stack[-1][1] == level:
-                    value = merge(stack.pop()[0], value, level)
-                    level *= 2
-                stack.append((value, level))
-        return merge(stacks[0][0][0], stacks[1][0][0], orders)
+        piece = min(slots, 4 * LANES)
+        sums = [[None] * (2 * outer) for _ in range(8)]
+        for begin in range(0, slots, piece):
+            part = slice(begin, begin + piece)
+            z = (bin_buf[here, part].astype(F32) + 0.5) * (2.0 / NBIN) - 1.0
+            twice = z + z
+            alive = slot_index[:, part] < count
+            vx = jnp.where(alive, x_buf[here, part], 0.0)
+            vy = jnp.where(alive, y_buf[here, part], 0.0)
+            t2 = twice * z - 1.0
+            t4 = 2.0 * t2 * t2 - 1.0
+            t8 = 2.0 * t4 * t4 - 1.0
+            steps = [None, t8]
+            for a in range(2, outer):
+                steps.append(2.0 * t8 * steps[a - 1] - (1.0 if a == 2 else steps[a - 2]))
+            streams = [v if a == 0 else v * steps[a] for v in (vx, vy) for a in range(outer)]
+            before, at = None, None
+            for j in range(8):
+                if j == 1:
+                    before, at = 1.0, z
+                elif j > 1:
+                    before, at = at, twice * at - before
+                for i, stream in enumerate(streams):
+                    term = tile_sum(stream if j == 0 else stream * at)
+                    sums[j][i] = term if sums[j][i] is None else sums[j][i] + term
+        values, distance = [value for row in sums for value in row], 1
+        while len(values) > 1:
+            values = [merge(p, q, distance) for p, q in zip(values[::2], values[1::2])]
+            distance *= 2
+        return values[0]
 
     def chunk(j, carry):
         first = pl.multiple_of(j * 8, 8)
@@ -178,7 +206,7 @@
         divisor = jnp.where(
             low_half, count_buf[pl.ds(first, 8), :], count_buf[pl.ds(second, 8), :]
         )
-        moments = total * scale / divisor
+        moments = total / divisor
         now_buf[t, j] = moments
         dom_buf[d, j] = moments
         for o in range(1, sections):
@@ -260,7 +288,9 @@
         past_here().wait()
 
     stored = past_buf[...].reshape(own * bunches, width)
-    convolved = dot3(w_past, split(stored))
+    for copy in loads[5:]:
+        copy.wait()
+    convolved = dot3(split(dot3(w_past, split(stored))), split(to_raw_in[...]))
 
     whole(now_buf, now_send, now_recv).wait_recv()
     gathered = now_buf[...].reshape(sections, half, LANES)
@@ -273,9 +303,8 @@
     conv_buf[d] = jnp.concatenate([convolved[:half], convolved[half:]], axis=1)
     dom_copies(conv_buf, conv_send, conv_recv)
 
-    for copy in loads[5:]:
-        copy.wait()
     to_kick = dot3(split(wake_in[...]), split(basis_buf[...]))
+    to_kick = dot3(split(to_moments_in[...]), split(to_kick))
     to_kick = jnp.concatenate([to_kick, to_kick], axis=0)
     to_kick = split(to_kick)
     angle = phase_in[...]
@@ -289,7 +318,7 @@
     summed = dom_buf[0]
     for i in range(1, doms):
         summed = summed + dom_buf[i]
-    summed = summed.reshape(half, LANES)
+    summed = dot3(split(summed.reshape(half, LANES)), split(to_both_in[...]))
     out[bunches : bunches + half, 0:width] = summed[:, :width]
     out[bunches + half : 2 * bunches, 0:width] = summed[:, width:]
 
@@ -359,7 +388,7 @@
     table = pl.pallas_call(
         functools.partial(moments_kernel, sections, doms, orders),
         out_shape=jax.ShapeDtypeStruct((2 * bunches + 8, 2 * NBIN), F32),
-        in_specs=[hbm] * 7,
+        in_specs=[hbm] * 10,
         out_specs=vmem,
         scratch_shapes=[
             pltpu.VMEM((bunches, slots), F32),
@@ -369,6 +398,9 @@
             pltpu.VMEM(wake_lags.shape, F32),
             pltpu.VMEM((width, width), F32),
             pltpu.VMEM((1, 2), F32),
+            pltpu.VMEM((width, width), F32),
+            pltpu.VMEM((width, width), F32),
+            pltpu.VMEM((2 * width, 2 * width), F32),
             pltpu.VMEM((pad + lag_rows, LANES), F32),
             pltpu.VMEM((width, 2 * NBIN), F32),
             pltpu.VMEM((bunches, LANES), F32),
@@ -376,7 +408,7 @@
             pltpu.VMEM((own, bunches, width), F32),
             pltpu.VMEM((doms, chunks, 8, LANES), F32),
             pltpu.VMEM((doms, half, LANES), F32),
-            dma((8,)),
+            dma((11,)),
             dma((sections - 1,)),
             dma((own,)),
             dma((6,)),
@@ -393,6 +425,7 @@
         wake_lags,
         wake_matrix,
         adjust_phase.reshape(1, -1),
+        *[jnp.asarray(m) for m in plane_maps(orders)],
     )
     return pl.pallas_call(
         track_kernel,

time: 37.4 us -> 20.1 us (0.54)
  Pallas kernels: 35.6 us -> 18.4 us
    pallas_call x1, Pallas kernels: 34.4 us -> 17.2 us  [local(): pl.pallas_call(functools.partial(moments_kernel, sections, doms, orders),...]
where the time goes in v4:
time: 20.1 us; the launch traced here: 19.9 us
  Pallas kernels  18.4 us (92%)
  local copies, waits for them, and re-layouts  0.91 us (5%)
  between operations  0.68 us (3%)
    pallas_call x1, Pallas kernels, local(): pl.pallas_call(functools.partial(moments_kernel, sections, doms, orders),...  17.2 us
    pallas_call x1, Pallas kernels, local(): pl.pallas_call(track_kernel, out_shape=(jax.ShapeDtypeStruct(particles.sh...  1.17 us
    unnamed x6, local copies, waits for them, and re-layouts  0.91 us

profile of v4, /device:TPU:0, one launch (start us, length us, event | category | flops | bytes accessed | tf_op | source)
XLA Modules:
  0.0 19.9 jit_solution(8541540049583643594)
XLA Ops:
  0.6 0.0 copy-start
  0.6 0.0 copy-start.1
  0.7 17.2 %moments.1.table = f32[136,256]{1,0:T(8,128)} custom-call(f32[4,64,1024]{2,1,0:T(8,128)} %particles.3, s32[64,1024]{1,0:T(8,128)} %bins.3, s32[1,64]{1,0:T(1,128)} %bitcast.2, f32[2,64,64]{2,1,0:T(8,128)} %past.1, f32[1535]{0:T(1024)} %lags.1, f32[64,64]{1,0:T(8,128)} %wake.1, f32[1,2]{1,0:T(1,128)} %bitcast.3, f32[64,64]{1,0:T(8,128)} %constant.6.clone.to_moments, ...), custom_call_target="tpu_custom_call" | custom-call | tf_op jit(solution)/shard_map/moments/pallas_call | solution.py:388
  17.8 0.0 copy-done
  17.9 0.0 copy-done.1
  17.9 0.0 copy-start.2
  17.9 0.9 %copy-done.2 = f32[136,256]{1,0:T(8,128)S(1)} copy-done((f32[136,256]{1,0:T(8,128)S(1)}, f32[136,256]{1,0:T(8,128)}, u32[]{:S(2)}) %copy-start.2) | copy-done | bytes 139288
  18.8 1.2 %track.1 = (f32[4,64,1024]{2,1,0:T(8,128)}, f32[64,64]{1,0:T(8,128)}) custom-call(f32[4,64,1024]{2,1,0:T(8,128)S(1)} %copy-done, s32[64,1024]{1,0:T(8,128)S(1)} %copy-done.1, f32[136,256]{1,0:T(8,128)S(1)} %copy-done.2), custom_call_target="tpu_custom_call" | custom-call | tf_op jit(solution)/shard_map/track/pallas_call | solution.py:430
Async XLA Ops:
  0.6 17.2 %copy-start = (f32[4,64,1024]{2,1,0:T(8,128)S(1)}, f32[4,64,1024]{2,1,0:T(8,128)}, u32[]{:S(2)}) copy-start(f32[4,64,1024]{2,1,0:T(8,128)} %particles.3) | copy-start | bytes 3145732
  0.6 17.2 %copy-start.1 = (s32[64,1024]{1,0:T(8,128)S(1)}, s32[64,1024]{1,0:T(8,128)}, u32[]{:S(2)}) copy-start(s32[64,1024]{1,0:T(8,128)} %bins.3) | copy-start | bytes 786436
  17.9 0.9 %copy-start.2 = (f32[136,256]{1,0:T(8,128)S(1)}, f32[136,256]{1,0:T(8,128)}, u32[]{:S(2)}) copy-start(f32[136,256]{1,0:T(8,128)} %moments.1.table) | copy-start | bytes 417796

commit v5 on v4

--- a/solution.py
+++ b/solution.py
@@ -33,9 +33,18 @@
     return lax.broadcasted_iota(jnp.int32, (rows, LANES), 1)
 
 
-def merge(a, b, distance):
-    low = (lane_iota(a.shape[0]) & distance) == 0
-    return jnp.where(low, a, b) + pltpu.roll(jnp.where(low, b, a), distance, 1)
+def dot_t(a, b):
+    return lax.dot_general(a, b, (((1,), (1,)), ((), ())), preferred_element_type=F32)
+
+
+def dot3_t(a_parts, b_parts):
+    (ah, al), (bh, bl) = a_parts, b_parts
+    return dot_t(ah, bh) + (dot_t(ah, bl) + dot_t(al, bh))
+
+
+def merge(a, b, distance, axis):
+    low = (lax.broadcasted_iota(jnp.int32, a.shape, axis) & distance) == 0
+    return jnp.where(low, a, b) + pltpu.roll(jnp.where(low, b, a), distance, axis)
 
 
 def product_basis(orders):
@@ -56,29 +65,23 @@
     for c in range(2):
         for j in range(8):
             for a in range(outer):
-                both[(j * 2 + c) * outer + a, c * orders : (c + 1) * orders] = one[j * outer + a]
-    twice = np.kron(np.eye(2), both)
-    return [m.astype(np.float32) for m in (both, np.linalg.inv(both), twice)]
-
-
-def tile_sum(a):
-    parts = [a[:, i : i + LANES] for i in range(0, a.shape[1], LANES)]
-    while len(parts) > 1:
-        parts = [p + q for p, q in zip(parts[::2], parts[1::2])] + parts[len(parts) & ~1 :]
-    return parts[0]
+                row = (j % 2) * orders + ((j // 2) * 2 + c) * outer + a
+                both[row, c * orders : (c + 1) * orders] = one[j * outer + a]
+    return both.astype(np.float32), np.linalg.inv(both).T.astype(np.float32)
 
 
 def moments_kernel(
     sections, doms, orders,
-    particles, bins, counts, past, lags, wake, phase, to_moments, to_raw, to_both,
+    particles, bins, counts, past, lags, wake, phase, to_moments, to_raw,
     out,
-    x_buf, y_buf, bin_buf, count_in, lag_in, wake_in, phase_in, to_moments_in, to_raw_in, to_both_in, e_buf, basis_buf, count_buf,
+    x_buf, y_buf, bin_buf, count_in, lag_in, wake_in, phase_in, to_moments_in, to_raw_in, e_buf, basis_buf,
+    stream_buf, twice_buf, poly_buf,
     now_buf, past_buf, dom_buf, conv_buf,
     load_sem, past_send, past_recv, pair_sem,
 ):
     bunches = counts.shape[1]
-    half = bunches // 2
-    chunks = half // 8
+    half = orders
+    chunks = 4
     width = 2 * orders
     bunches_all = bunches * sections
     own = 2 * sections // doms
@@ -105,7 +108,6 @@
         (phase, phase_in),
         (to_moments, to_moments_in),
         (to_raw, to_raw_in),
-        (to_both, to_both_in),
     ]
     loads = [
         pltpu.make_async_copy(src, dst, load_sem.at[i]) for i, (src, dst) in enumerate(pairs)
@@ -142,14 +144,6 @@
         following = following - np.float32((k + 1) / (k + 2)) * previous
         previous, current = current, following
 
-    loads[0].wait()
-    eye = lax.broadcasted_iota(jnp.int32, (bunches, bunches), 0) == lax.broadcasted_iota(
-        jnp.int32, (bunches, bunches), 1
-    )
-    count_f = count_in[...].astype(F32)
-    column = jnp.sum(jnp.where(eye, count_f, 0.0), axis=1, keepdims=True)
-    count_buf[...] = jnp.broadcast_to(column, (bunches, LANES))
-
     pl.semaphore_wait(barrier, sections - 1 + doms - 1)
 
     @pl.when(owned)
@@ -157,56 +151,69 @@
         for o in range(1, sections):
             past_copy(o).start()
 
-    for copy in loads[1:4]:
+    for copy in loads[0:4]:
         copy.wait()
     slots = x_buf.shape[1]
-    slot_index = d * slots + lax.broadcasted_iota(jnp.int32, (8, slots), 1)
-    low_half = lane_iota(8) < width
-
+    deep = slots // 2
     outer = orders // 8
-
-    def group_sums(first):
-        here = pl.ds(first, 8)
-        count = count_buf[here, 0:1].astype(jnp.int32)
-        piece = min(slots, 4 * LANES)
-        sums = [[None] * (2 * outer) for _ in range(8)]
-        for begin in range(0, slots, piece):
-            part = slice(begin, begin + piece)
-            z = (bin_buf[here, part].astype(F32) + 0.5) * (2.0 / NBIN) - 1.0
-            twice = z + z
-            alive = slot_index[:, part] < count
-            vx = jnp.where(alive, x_buf[here, part], 0.0)
-            vy = jnp.where(alive, y_buf[here, part], 0.0)
-            t2 = twice * z - 1.0
-            t4 = 2.0 * t2 * t2 - 1.0
-            t8 = 2.0 * t4 * t4 - 1.0
-            steps = [None, t8]
-            for a in range(2, outer):
-                steps.append(2.0 * t8 * steps[a - 1] - (1.0 if a == 2 else steps[a - 2]))
-            streams = [v if a == 0 else v * steps[a] for v in (vx, vy) for a in range(outer)]
-            before, at = None, None
-            for j in range(8):
-                if j == 1:
-                    before, at = 1.0, z
-                elif j > 1:
-                    before, at = at, twice * at - before
-                for i, stream in enumerate(streams):
-                    term = tile_sum(stream if j == 0 else stream * at)
-                    sums[j][i] = term if sums[j][i] is None else sums[j][i] + term
-        values, distance = [value for row in sums for value in row], 1
-        while len(values) > 1:
-            values = [merge(p, q, distance) for p, q in zip(values[::2], values[1::2])]
-            distance *= 2
-        return values[0]
-
-    def chunk(j, carry):
-        first = pl.multiple_of(j * 8, 8)
-        second = pl.multiple_of(j * 8 + half, 8)
-        total = merge(group_sums(first), group_sums(second), width)
-        divisor = jnp.where(
-            low_half, count_buf[pl.ds(first, 8), :], count_buf[pl.ds(second, 8), :]
-        )
-        moments = total / divisor
+    count = jnp.concatenate([count_in[...], count_in[...]], axis=1)
+    slot_index = (
+        d * slots
+        + jnp.where(lane_iota(LANES) < bunches, 0, deep)
+        + lax.broadcasted_iota(jnp.int32, (LANES, LANES), 0)
+    )
+
+    def upright(ref, first):
+        return jnp.concatenate(
+            [ref[:, first : first + LANES], ref[:, deep + first : deep + first + LANES]], axis=0
+        ).T
+
+    for first in range(0, deep, LANES):
+        here = slice(first, first + LANES)
+        z = (upright(bin_buf, first).astype(F32) + 0.5) * (2.0 / NBIN) - 1.0
+        twice = z + z
+        t2 = twice * z - 1.0
+        t4 = 2.0 * t2 * t2 - 1.0
+        t8 = 2.0 * t4 * t4 - 1.0
+        twice_buf[here, :] = twice
+        poly_buf[0, here, :] = jnp.ones_like(z)
+        poly_buf[1, here, :] = z
+        steps = [None, t8]
+        for a in range(2, outer):
+            steps.append(2.0 * t8 * steps[a - 1] - (1.0 if a == 2 else steps[a - 2]))
+        alive = slot_index + first < count
+        for c, ref in enumerate((x_buf, y_buf)):
+            v = jnp.where(alive, upright(ref, first), 0.0)
+            for a in range(outer):
+                stream_buf[c * outer + a, here, :] = v if a == 0 else v * steps[a]
+
+    unroll = 4
+    count_f = count.astype(F32)
+    for j in range(chunks):
+
+        def rows_step(i, sums):
+            sums = list(sums)
+            for u in range(unroll):
+                here = pl.ds(pl.multiple_of((i * unroll + u) * 8, 8), 8)
+                even, odd = poly_buf[0, here, :], poly_buf[1, here, :]
+                if j > 0:
+                    twice = twice_buf[here, :]
+                    even = twice * odd - even
+                    odd = twice * even - odd
+                    if j < chunks - 1:
+                        poly_buf[0, here, :] = even
+                        poly_buf[1, here, :] = odd
+                for n in range(2 * outer):
+                    stream = stream_buf[n, here, :]
+                    sums[n] = sums[n] + (stream if j == 0 else stream * even)
+                    sums[2 * outer + n] = sums[2 * outer + n] + stream * odd
+            return tuple(sums)
+
+        zero = jnp.zeros((8, LANES), F32)
+        values = lax.fori_loop(0, deep // (8 * unroll), rows_step, (zero,) * (4 * outer))
+        for distance in (1, 2, 4):
+            values = [merge(p, q, distance, 0) for p, q in zip(values[::2], values[1::2])]
+        moments = merge(values[0], values[1], width, 1) / count_f
         now_buf[t, j] = moments
         dom_buf[d, j] = moments
         for o in range(1, sections):
@@ -215,9 +222,6 @@
                 send_sem=now_send, recv_sem=now_recv,
                 device_id=(lax.rem(t + o, sections), d), device_id_type=MESH,
             ).start()
-        return carry
-
-    lax.fori_loop(0, chunks, chunk, 0)
 
     def dom_copies(ref, send_sem, recv_sem):
         for o in range(1, doms):
@@ -262,17 +266,21 @@
             )
 
         turned_rows = [rolled(tile_first + m) for m in range(-1, tiles)]
-        return jnp.concatenate(
-            [
-                jnp.where(source >= target, turned_rows[m + 1], turned_rows[m])
-                for m in range(tiles)
-            ],
-            axis=1,
-        )
-
-    w_now = split(toeplitz(2 * bunches_all // LANES, bunches_all // LANES))
+        return [
+            jnp.where(source >= target, turned_rows[m + 1], turned_rows[m]) for m in range(tiles)
+        ]
+
+    low = source < bunches
+    above, below = [], []
+    for tile in toeplitz(2 * bunches_all // LANES, bunches_all // LANES):
+        swapped = pltpu.roll(tile, LANES // 2, 1)
+        above += [jnp.where(low, tile, 0.0), jnp.where(low, swapped, 0.0)]
+        below += [jnp.where(low, 0.0, swapped), jnp.where(low, 0.0, tile)]
+    w_now = split(
+        jnp.concatenate([jnp.concatenate(above, axis=1), jnp.concatenate(below, axis=1)], axis=0)
+    )
     past_tiles = own * bunches // LANES
-    w_past = split(toeplitz(d * past_tiles, past_tiles))
+    w_past = split(jnp.concatenate(toeplitz(d * past_tiles, past_tiles), axis=1))
 
     for s in range(own):
         @pl.when(lax.rem(d * own + s, sections) != t)
@@ -290,23 +298,19 @@
     stored = past_buf[...].reshape(own * bunches, width)
     for copy in loads[5:]:
         copy.wait()
-    convolved = dot3(split(dot3(w_past, split(stored))), split(to_raw_in[...]))
+    raw = dot3_t(split(to_raw_in[...]), split(dot3(w_past, split(stored))))
+    convolved = jnp.concatenate([raw[:half], raw[half:]], axis=1)
 
     whole(now_buf, now_send, now_recv).wait_recv()
-    gathered = now_buf[...].reshape(sections, half, LANES)
-    lower = lane_iota(half)[None] < width
-    spread = jnp.concatenate(
-        [jnp.where(lower, gathered, 0.0), jnp.where(lower, 0.0, gathered)], axis=1
-    ).reshape(bunches_all, LANES)
-    both = dot3(w_now, split(spread))
-    convolved = convolved + (both[:, :width] + both[:, width:])
-    conv_buf[d] = jnp.concatenate([convolved[:half], convolved[half:]], axis=1)
+    gathered = jnp.concatenate(
+        [now_buf[i].reshape(half, LANES) for i in range(sections)], axis=1
+    )
+    conv_buf[d] = convolved + dot3_t(split(gathered), w_now)
     dom_copies(conv_buf, conv_send, conv_recv)
 
     to_kick = dot3(split(wake_in[...]), split(basis_buf[...]))
     to_kick = dot3(split(to_moments_in[...]), split(to_kick))
-    to_kick = jnp.concatenate([to_kick, to_kick], axis=0)
-    to_kick = split(to_kick)
+    to_kick = split(to_kick[:half]), split(to_kick[half:])
     angle = phase_in[...]
     cosine, sine = jnp.cos(angle), jnp.sin(angle)
     for plane in range(2):
@@ -318,9 +322,14 @@
     summed = dom_buf[0]
     for i in range(1, doms):
         summed = summed + dom_buf[i]
-    summed = dot3(split(summed.reshape(half, LANES)), split(to_both_in[...]))
-    out[bunches : bunches + half, 0:width] = summed[:, :width]
-    out[bunches + half : 2 * bunches, 0:width] = summed[:, width:]
+    def from_packed(packed, maps):
+        turned = packed.T
+        return dot3(split(turned[:bunches]), maps[0]) + dot3(split(turned[bunches:]), maps[1])
+
+    to_moments_parts = split(to_moments_in[0:half, :]), split(to_moments_in[half:width, :])
+    out[bunches : 2 * bunches, 0:width] = from_packed(
+        summed.reshape(half, LANES), to_moments_parts
+    )
 
     @pl.when(owned)
     def _():
@@ -335,9 +344,7 @@
     total = conv_buf[0]
     for i in range(1, doms):
         total = total + conv_buf[i]
-    lower = lane_iota(half) < width
-    total = jnp.concatenate([jnp.where(lower, total, 0.0), jnp.where(lower, 0.0, total)], axis=0)
-    out[0:bunches, :] = dot3(split(total), to_kick)
+    out[0:bunches, :] = from_packed(total, to_kick)
     conv_wait.wait_send()
 
 
@@ -376,8 +383,8 @@
     _, bunches, slots = particles.shape
     width = wake_matrix.shape[0]
     orders = width // 2
-    half = bunches // 2
-    chunks = half // 8
+    half = orders
+    chunks = 4
     bunches_all = bunches * sections
     own = 2 * sections // doms
     lag_rows = bunches_all // 32
@@ -388,7 +395,7 @@
     table = pl.pallas_call(
         functools.partial(moments_kernel, sections, doms, orders),
         out_shape=jax.ShapeDtypeStruct((2 * bunches + 8, 2 * NBIN), F32),
-        in_specs=[hbm] * 10,
+        in_specs=[hbm] * 9,
         out_specs=vmem,
         scratch_shapes=[
             pltpu.VMEM((bunches, slots), F32),
@@ -400,15 +407,16 @@
             pltpu.VMEM((1, 2), F32),
             pltpu.VMEM((width, width), F32),
             pltpu.VMEM((width, width), F32),
-            pltpu.VMEM((2 * width, 2 * width), F32),
             pltpu.VMEM((pad + lag_rows, LANES), F32),
             pltpu.VMEM((width, 2 * NBIN), F32),
-            pltpu.VMEM((bunches, LANES), F32),
+            pltpu.VMEM((width // 8, slots // 2, LANES), F32),
+            pltpu.VMEM((slots // 2, LANES), F32),
+            pltpu.VMEM((2, slots // 2, LANES), F32),
             pltpu.VMEM((sections, chunks, 8, LANES), F32),
             pltpu.VMEM((own, bunches, width), F32),
             pltpu.VMEM((doms, chunks, 8, LANES), F32),
             pltpu.VMEM((doms, half, LANES), F32),
-            dma((11,)),
+            dma((10,)),
             dma((sections - 1,)),
             dma((own,)),
             dma((6,)),

time: 20.1 us -> 19.8 us (0.985)
  Pallas kernels: 18.4 us -> 18 us
    pallas_call x1, Pallas kernels: 17.2 us -> 16.9 us  [local(): pl.pallas_call(functools.partial(moments_kernel, sections, doms, orders),...]
where the time goes in v5:
time: 19.8 us; the launch traced here: 19.6 us
  Pallas kernels  18 us (91%)
  local copies, waits for them, and re-layouts  0.91 us (5%)
  between operations  0.68 us (3%)
    pallas_call x1, Pallas kernels, local(): pl.pallas_call(functools.partial(moments_kernel, sections, doms, orders),...  16.9 us
    pallas_call x1, Pallas kernels, local(): pl.pallas_call(track_kernel, out_shape=(jax.ShapeDtypeStruct(particles.sh...  1.17 us
    unnamed x6, local copies, waits for them, and re-layouts  0.91 us

profile of v5, /device:TPU:0, one launch (start us, length us, event | category | flops | bytes accessed | tf_op | source)
XLA Modules:
  0.0 19.6 jit_solution(113686437460749206)
XLA Ops:
  0.6 0.0 copy-start
  0.6 0.0 copy-start.1
  0.7 16.9 %moments.1.table = f32[136,256]{1,0:T(8,128)} custom-call(f32[4,64,1024]{2,1,0:T(8,128)} %particles.3, s32[64,1024]{1,0:T(8,128)} %bins.3, s32[1,64]{1,0:T(1,128)} %bitcast.2, f32[2,64,64]{2,1,0:T(8,128)} %past.1, f32[1535]{0:T(1024)} %lags.1, f32[64,64]{1,0:T(8,128)} %wake.1, f32[1,2]{1,0:T(1,128)} %bitcast.3, f32[64,64]{1,0:T(8,128)} %constant.4.clone.to_moments, ...), custom_call_target="tpu_custom_call" | custom-call | tf_op jit(solution)/shard_map/moments/pallas_call | solution.py:395
  17.5 0.0 copy-done
  17.5 0.0 copy-done.1
  17.5 0.0 copy-start.2
  17.5 0.9 %copy-done.2 = f32[136,256]{1,0:T(8,128)S(1)} copy-done((f32[136,256]{1,0:T(8,128)S(1)}, f32[136,256]{1,0:T(8,128)}, u32[]{:S(2)}) %copy-start.2) | copy-done | bytes 139288
  18.4 1.2 %track.1 = (f32[4,64,1024]{2,1,0:T(8,128)}, f32[64,64]{1,0:T(8,128)}) custom-call(f32[4,64,1024]{2,1,0:T(8,128)S(1)} %copy-done, s32[64,1024]{1,0:T(8,128)S(1)} %copy-done.1, f32[136,256]{1,0:T(8,128)S(1)} %copy-done.2), custom_call_target="tpu_custom_call" | custom-call | tf_op jit(solution)/shard_map/track/pallas_call | solution.py:438
Async XLA Ops:
  0.6 16.9 %copy-start = (f32[4,64,1024]{2,1,0:T(8,128)S(1)}, f32[4,64,1024]{2,1,0:T(8,128)}, u32[]{:S(2)}) copy-start(f32[4,64,1024]{2,1,0:T(8,128)} %particles.3) | copy-start | bytes 3145732
  0.6 16.9 %copy-start.1 = (s32[64,1024]{1,0:T(8,128)S(1)}, s32[64,1024]{1,0:T(8,128)}, u32[]{:S(2)}) copy-start(s32[64,1024]{1,0:T(8,128)} %bins.3) | copy-start | bytes 786436
  17.5 0.9 %copy-start.2 = (f32[136,256]{1,0:T(8,128)S(1)}, f32[136,256]{1,0:T(8,128)}, u32[]{:S(2)}) copy-start(f32[136,256]{1,0:T(8,128)} %moments.1.table) | copy-start | bytes 417796

commit v6 on v5

--- a/solution.py
+++ b/solution.py
@@ -76,7 +76,7 @@
     out,
     x_buf, y_buf, bin_buf, count_in, lag_in, wake_in, phase_in, to_moments_in, to_raw_in, e_buf, basis_buf,
     stream_buf, twice_buf, poly_buf,
-    now_buf, past_buf, dom_buf, conv_buf,
+    now_buf, past_in, past_mine, past_buf, part_mine, part_buf, share_mine, share_buf, dom_buf, conv_buf,
     load_sem, past_send, past_recv, pair_sem,
 ):
     bunches = counts.shape[1]
@@ -87,7 +87,11 @@
     own = 2 * sections // doms
     t = lax.axis_index("train")
     d = lax.axis_index("dom")
-    now_send, now_recv, dom_send, dom_recv, conv_send, conv_recv = [pair_sem.at[i] for i in range(6)]
+    part_sems, now_sems, dom_sems, share_sems, conv_sems = [
+        (pair_sem.at[2 * i], pair_sem.at[2 * i + 1]) for i in range(5)
+    ]
+    pieces = doms // chunks
+    piece_rows = half // doms
 
     barrier = pltpu.get_barrier_semaphore()
     for o in range(1, sections):
@@ -122,13 +126,13 @@
 
     def past_copy(o):
         return pltpu.make_async_remote_copy(
-            src_ref=past.at[turn], dst_ref=past_buf.at[slot],
+            src_ref=past_mine, dst_ref=past_buf.at[slot],
             send_sem=past_send.at[o - 1], recv_sem=past_recv.at[slot],
             device_id=(lax.rem(t + o, sections), d), device_id_type=MESH,
         )
 
     def past_here():
-        return pltpu.make_async_copy(past.at[turn], past_buf.at[slot], load_sem.at[len(pairs)])
+        return pltpu.make_async_copy(past.at[turn], past_in, load_sem.at[len(pairs)])
 
     @pl.when(owned)
     def _():
@@ -148,6 +152,11 @@
 
     @pl.when(owned)
     def _():
+        past_here().wait()
+        block = past_in[...]
+        block = jnp.concatenate([block[: bunches // 2], block[bunches // 2 :]], axis=1)
+        past_mine[...] = block
+        past_buf[slot] = block
         for o in range(1, sections):
             past_copy(o).start()
 
@@ -187,6 +196,28 @@
             for a in range(outer):
                 stream_buf[c * outer + a, here, :] = v if a == 0 else v * steps[a]
 
+    def dom_copies(ref, sems):
+        for o in range(1, doms):
+            pltpu.make_async_remote_copy(
+                src_ref=ref.at[d], dst_ref=ref.at[d], send_sem=sems[0], recv_sem=sems[1],
+                device_id=(t, lax.rem(d + o, doms)), device_id_type=MESH,
+            ).start()
+
+    def to_piece(mine, buf, sems, e):
+        @pl.when(d != e)
+        def _():
+            pltpu.make_async_remote_copy(
+                src_ref=mine.at[e], dst_ref=buf.at[d], send_sem=sems[0], recv_sem=sems[1],
+                device_id=(t, e), device_id_type=MESH,
+            ).start()
+
+    def whole(ref, sems):
+        part = ref.at[pl.ds(0, ref.shape[0] - 1)]
+        return pltpu.make_async_remote_copy(
+            src_ref=part, dst_ref=part, send_sem=sems[0], recv_sem=sems[1],
+            device_id=(t, d), device_id_type=MESH,
+        )
+
     unroll = 4
     count_f = count.astype(F32)
     for j in range(chunks):
@@ -213,31 +244,40 @@
         values = lax.fori_loop(0, deep // (8 * unroll), rows_step, (zero,) * (4 * outer))
         for distance in (1, 2, 4):
             values = [merge(p, q, distance, 0) for p, q in zip(values[::2], values[1::2])]
-        moments = merge(values[0], values[1], width, 1) / count_f
-        now_buf[t, j] = moments
-        dom_buf[d, j] = moments
-        for o in range(1, sections):
-            pltpu.make_async_remote_copy(
-                src_ref=now_buf.at[t, j], dst_ref=now_buf.at[t, j],
-                send_sem=now_send, recv_sem=now_recv,
-                device_id=(lax.rem(t + o, sections), d), device_id_type=MESH,
-            ).start()
-
-    def dom_copies(ref, send_sem, recv_sem):
-        for o in range(1, doms):
-            pltpu.make_async_remote_copy(
-                src_ref=ref.at[d], dst_ref=ref.at[d], send_sem=send_sem, recv_sem=recv_sem,
-                device_id=(t, lax.rem(d + o, doms)), device_id_type=MESH,
-            ).start()
-
-    def whole(ref, send_sem, recv_sem):
-        part = ref.at[pl.ds(0, ref.shape[0] - 1)]
-        return pltpu.make_async_remote_copy(
-            src_ref=part, dst_ref=part, send_sem=send_sem, recv_sem=recv_sem,
-            device_id=(t, d), device_id_type=MESH,
-        )
-
-    dom_copies(dom_buf, dom_send, dom_recv)
+        moments = merge(values[0], values[1], width, 1)
+        for i in range(pieces):
+            e = j * pieces + i
+            part_mine[e] = moments[i * piece_rows : (i + 1) * piece_rows]
+            to_piece(part_mine, part_buf, part_sems, e)
+
+    for copy in loads[5:]:
+        copy.wait()
+    to_kick = dot3(split(wake_in[...]), split(basis_buf[...]))
+    to_kick = dot3(split(to_moments_in[...]), split(to_kick))
+    to_kick = split(to_kick[:half]), split(to_kick[half:])
+    angle = phase_in[...]
+    cosine, sine = jnp.cos(angle), jnp.sin(angle)
+    for plane in range(2):
+        row = 2 * bunches + 2 * plane
+        out[row : row + 1, :] = jnp.broadcast_to(cosine[:, plane : plane + 1], (1, 2 * NBIN))
+        out[row + 1 : row + 2, :] = jnp.broadcast_to(sine[:, plane : plane + 1], (1, 2 * NBIN))
+
+    part_buf[d] = part_mine[d]
+    part_wait = whole(part_buf, part_sems)
+    part_wait.wait_recv()
+    reduced = part_buf[0]
+    for i in range(1, doms):
+        reduced = reduced + part_buf[i]
+    reduced = reduced / count_f
+    now_buf[t] = reduced
+    dom_buf[d] = reduced
+    for o in range(1, sections):
+        pltpu.make_async_remote_copy(
+            src_ref=now_buf.at[t], dst_ref=now_buf.at[t],
+            send_sem=now_sems[0], recv_sem=now_sems[1],
+            device_id=(lax.rem(t + o, sections), d), device_id_type=MESH,
+        ).start()
+    dom_copies(dom_buf, dom_sems)
 
     loads[4].wait()
     rows = bunches_all // 32
@@ -286,49 +326,43 @@
         @pl.when(lax.rem(d * own + s, sections) != t)
         def _():
             pltpu.make_async_remote_copy(
-                src_ref=past.at[0], dst_ref=past_buf.at[s],
+                src_ref=past_mine, dst_ref=past_buf.at[s],
                 send_sem=past_send.at[0], recv_sem=past_recv.at[s],
                 device_id=(t, d), device_id_type=MESH,
             ).wait_recv()
 
-    @pl.when(owned)
-    def _():
-        past_here().wait()
-
-    stored = past_buf[...].reshape(own * bunches, width)
-    for copy in loads[5:]:
-        copy.wait()
+    stored = jnp.concatenate(
+        [past_buf[i][:, side * width : (side + 1) * width] for i in range(own) for side in range(2)],
+        axis=0,
+    )
     raw = dot3_t(split(to_raw_in[...]), split(dot3(w_past, split(stored))))
     convolved = jnp.concatenate([raw[:half], raw[half:]], axis=1)
 
-    whole(now_buf, now_send, now_recv).wait_recv()
-    gathered = jnp.concatenate(
-        [now_buf[i].reshape(half, LANES) for i in range(sections)], axis=1
-    )
-    conv_buf[d] = convolved + dot3_t(split(gathered), w_now)
-    dom_copies(conv_buf, conv_send, conv_recv)
-
-    to_kick = dot3(split(wake_in[...]), split(basis_buf[...]))
-    to_kick = dot3(split(to_moments_in[...]), split(to_kick))
-    to_kick = split(to_kick[:half]), split(to_kick[half:])
-    angle = phase_in[...]
-    cosine, sine = jnp.cos(angle), jnp.sin(angle)
-    for plane in range(2):
-        row = 2 * bunches + 2 * plane
-        out[row : row + 1, :] = jnp.broadcast_to(cosine[:, plane : plane + 1], (1, 2 * NBIN))
-        out[row + 1 : row + 2, :] = jnp.broadcast_to(sine[:, plane : plane + 1], (1, 2 * NBIN))
-    dom_wait = whole(dom_buf, dom_send, dom_recv)
+    for e in range(doms):
+        share_mine[e] = convolved[e * piece_rows : (e + 1) * piece_rows]
+        to_piece(share_mine, share_buf, share_sems, e)
+    share_buf[d] = share_mine[d]
+
+    now_wait = whole(now_buf, now_sems)
+    now_wait.wait_recv()
+    gathered = jnp.concatenate([now_buf[i] for i in range(sections)], axis=1)
+    convolved = dot3_t(split(gathered), w_now)
+    share_wait = whole(share_buf, share_sems)
+    share_wait.wait_recv()
+    for i in range(doms):
+        convolved = convolved + share_buf[i]
+    conv_buf[d] = convolved
+    dom_copies(conv_buf, conv_sems)
+
+    dom_wait = whole(dom_buf, dom_sems)
     dom_wait.wait_recv()
-    summed = dom_buf[0]
-    for i in range(1, doms):
-        summed = summed + dom_buf[i]
     def from_packed(packed, maps):
         turned = packed.T
         return dot3(split(turned[:bunches]), maps[0]) + dot3(split(turned[bunches:]), maps[1])
 
     to_moments_parts = split(to_moments_in[0:half, :]), split(to_moments_in[half:width, :])
     out[bunches : 2 * bunches, 0:width] = from_packed(
-        summed.reshape(half, LANES), to_moments_parts
+        dom_buf[...].reshape(half, LANES), to_moments_parts
     )
 
     @pl.when(owned)
@@ -336,14 +370,12 @@
         for o in range(1, sections):
             past_copy(o).wait_send()
 
-    whole(now_buf, now_send, now_recv).wait_send()
-    dom_wait.wait_send()
-
-    conv_wait = whole(conv_buf, conv_send, conv_recv)
+    for copy in (part_wait, now_wait, dom_wait, share_wait):
+        copy.wait_send()
+
+    conv_wait = whole(conv_buf, conv_sems)
     conv_wait.wait_recv()
-    total = conv_buf[0]
-    for i in range(1, doms):
-        total = total + conv_buf[i]
+    total = conv_buf[...].reshape(half, LANES)
     out[0:bunches, :] = from_packed(total, to_kick)
     conv_wait.wait_send()
 
@@ -384,7 +416,6 @@
     width = wake_matrix.shape[0]
     orders = width // 2
     half = orders
-    chunks = 4
     bunches_all = bunches * sections
     own = 2 * sections // doms
     lag_rows = bunches_all // 32
@@ -412,14 +443,15 @@
             pltpu.VMEM((width // 8, slots // 2, LANES), F32),
             pltpu.VMEM((slots // 2, LANES), F32),
             pltpu.VMEM((2, slots // 2, LANES), F32),
-            pltpu.VMEM((sections, chunks, 8, LANES), F32),
-            pltpu.VMEM((own, bunches, width), F32),
-            pltpu.VMEM((doms, chunks, 8, LANES), F32),
-            pltpu.VMEM((doms, half, LANES), F32),
+            pltpu.VMEM((sections, half // doms, LANES), F32),
+            pltpu.VMEM((bunches, width), F32),
+            pltpu.VMEM((bunches // 2, 2 * width), F32),
+            pltpu.VMEM((own, bunches // 2, 2 * width), F32),
+            *[pltpu.VMEM((doms, half // doms, LANES), F32)] * 6,
             dma((10,)),
             dma((sections - 1,)),
             dma((own,)),
-            dma((6,)),
+            dma((10,)),
         ],
         compiler_params=pltpu.CompilerParams(
             collective_id=0, has_side_effects=True, vmem_limit_bytes=56 * 1024 * 1024

time: 19.8 us -> 20.6 us (1.040)
  Pallas kernels: 18 us -> 18.9 us
    pallas_call x1, Pallas kernels: 16.9 us -> 17.7 us  [local(): pl.pallas_call(functools.partial(moments_kernel, sections, doms, orders),...]
where the time goes in v6:
time: 20.6 us; the launch traced here: 20.5 us
  Pallas kernels  18.9 us (92%)
  local copies, waits for them, and re-layouts  0.91 us (4%)
  between operations  0.68 us (3%)
    pallas_call x1, Pallas kernels, local(): pl.pallas_call(functools.partial(moments_kernel, sections, doms, orders),...  17.7 us
    pallas_call x1, Pallas kernels, local(): pl.pallas_call(track_kernel, out_shape=(jax.ShapeDtypeStruct(particles.sh...  1.17 us
    unnamed x6, local copies, waits for them, and re-layouts  0.91 us

profile of v6, /device:TPU:0, one launch (start us, length us, event | category | flops | bytes accessed | tf_op | source)
XLA Modules:
  0.0 20.5 jit_solution(8794756257478272419)
XLA Ops:
  0.6 0.0 copy-start
  0.6 0.0 copy-start.1
  0.7 17.7 %moments.1.table = f32[136,256]{1,0:T(8,128)} custom-call(f32[4,64,1024]{2,1,0:T(8,128)} %particles.3, s32[64,1024]{1,0:T(8,128)} %bins.3, s32[1,64]{1,0:T(1,128)} %bitcast.2, f32[2,64,64]{2,1,0:T(8,128)} %past.1, f32[1535]{0:T(1024)} %lags.1, f32[64,64]{1,0:T(8,128)} %wake.1, f32[1,2]{1,0:T(1,128)} %bitcast.3, f32[64,64]{1,0:T(8,128)} %constant.4.clone.to_moments, ...), custom_call_target="tpu_custom_call" | custom-call | tf_op jit(solution)/shard_map/moments/pallas_call | solution.py:426
  18.4 0.0 copy-done
  18.4 0.0 copy-done.1
  18.4 0.0 copy-start.2
  18.4 0.9 %copy-done.2 = f32[136,256]{1,0:T(8,128)S(1)} copy-done((f32[136,256]{1,0:T(8,128)S(1)}, f32[136,256]{1,0:T(8,128)}, u32[]{:S(2)}) %copy-start.2) | copy-done | bytes 139288
  19.3 1.2 %track.1 = (f32[4,64,1024]{2,1,0:T(8,128)}, f32[64,64]{1,0:T(8,128)}) custom-call(f32[4,64,1024]{2,1,0:T(8,128)S(1)} %copy-done, s32[64,1024]{1,0:T(8,128)S(1)} %copy-done.1, f32[136,256]{1,0:T(8,128)S(1)} %copy-done.2), custom_call_target="tpu_custom_call" | custom-call | tf_op jit(solution)/shard_map/track/pallas_call | solution.py:470
Async XLA Ops:
  0.6 17.7 %copy-start = (f32[4,64,1024]{2,1,0:T(8,128)S(1)}, f32[4,64,1024]{2,1,0:T(8,128)}, u32[]{:S(2)}) copy-start(f32[4,64,1024]{2,1,0:T(8,128)} %particles.3) | copy-start | bytes 3145732
  0.6 17.7 %copy-start.1 = (s32[64,1024]{1,0:T(8,128)S(1)}, s32[64,1024]{1,0:T(8,128)}, u32[]{:S(2)}) copy-start(s32[64,1024]{1,0:T(8,128)} %bins.3) | copy-start | bytes 786436
  18.4 0.9 %copy-start.2 = (f32[136,256]{1,0:T(8,128)S(1)}, f32[136,256]{1,0:T(8,128)}, u32[]{:S(2)}) copy-start(f32[136,256]{1,0:T(8,128)} %moments.1.table) | copy-start | bytes 417796

commit v7 on v5

--- a/solution.py
+++ b/solution.py
@@ -76,8 +76,8 @@
     out,
     x_buf, y_buf, bin_buf, count_in, lag_in, wake_in, phase_in, to_moments_in, to_raw_in, e_buf, basis_buf,
     stream_buf, twice_buf, poly_buf,
-    now_buf, past_buf, dom_buf, conv_buf,
-    load_sem, past_send, past_recv, pair_sem,
+    now_buf, past_in, past_mine, past_buf, dom_buf, conv_buf,
+    load_sem, past_send, past_recv, now_send, now_recv, pair_sem,
 ):
     bunches = counts.shape[1]
     half = orders
@@ -87,7 +87,7 @@
     own = 2 * sections // doms
     t = lax.axis_index("train")
     d = lax.axis_index("dom")
-    now_send, now_recv, dom_send, dom_recv, conv_send, conv_recv = [pair_sem.at[i] for i in range(6)]
+    dom_send, dom_recv, conv_send, conv_recv = [pair_sem.at[i] for i in range(4)]
 
     barrier = pltpu.get_barrier_semaphore()
     for o in range(1, sections):
@@ -122,13 +122,13 @@
 
     def past_copy(o):
         return pltpu.make_async_remote_copy(
-            src_ref=past.at[turn], dst_ref=past_buf.at[slot],
+            src_ref=past_mine, dst_ref=past_buf.at[slot],
             send_sem=past_send.at[o - 1], recv_sem=past_recv.at[slot],
             device_id=(lax.rem(t + o, sections), d), device_id_type=MESH,
         )
 
     def past_here():
-        return pltpu.make_async_copy(past.at[turn], past_buf.at[slot], load_sem.at[len(pairs)])
+        return pltpu.make_async_copy(past.at[turn], past_in, load_sem.at[len(pairs)])
 
     @pl.when(owned)
     def _():
@@ -148,8 +148,18 @@
 
     @pl.when(owned)
     def _():
+        past_here().wait()
+        block = past_in[...]
+        block = jnp.concatenate([block[: bunches // 2], block[bunches // 2 :]], axis=1)
+        past_mine[...] = block
+        past_buf[slot] = block
         for o in range(1, sections):
             past_copy(o).start()
+
+    for i in range(1, sections):
+        @pl.when(t < i)
+        def _():
+            now_buf[i] = jnp.zeros(now_buf.shape[1:], F32)
 
     for copy in loads[0:4]:
         copy.wait()
@@ -217,11 +227,20 @@
         now_buf[t, j] = moments
         dom_buf[d, j] = moments
         for o in range(1, sections):
-            pltpu.make_async_remote_copy(
-                src_ref=now_buf.at[t, j], dst_ref=now_buf.at[t, j],
-                send_sem=now_send, recv_sem=now_recv,
-                device_id=(lax.rem(t + o, sections), d), device_id_type=MESH,
-            ).start()
+            @pl.when(t + o < sections)
+            def _():
+                pltpu.make_async_remote_copy(
+                    src_ref=now_buf.at[t, j], dst_ref=now_buf.at[t, j],
+                    send_sem=now_send.at[o - 1], recv_sem=now_recv.at[o - 1],
+                    device_id=(lax.rem(t + o, sections), d), device_id_type=MESH,
+                ).start()
+
+    def now_copy(o):
+        return pltpu.make_async_remote_copy(
+            src_ref=now_buf.at[t], dst_ref=now_buf.at[t],
+            send_sem=now_send.at[o - 1], recv_sem=now_recv.at[o - 1],
+            device_id=(lax.rem(t + o, sections), d), device_id_type=MESH,
+        )
 
     def dom_copies(ref, send_sem, recv_sem):
         for o in range(1, doms):
@@ -286,22 +305,25 @@
         @pl.when(lax.rem(d * own + s, sections) != t)
         def _():
             pltpu.make_async_remote_copy(
-                src_ref=past.at[0], dst_ref=past_buf.at[s],
+                src_ref=past_mine, dst_ref=past_buf.at[s],
                 send_sem=past_send.at[0], recv_sem=past_recv.at[s],
                 device_id=(t, d), device_id_type=MESH,
             ).wait_recv()
 
-    @pl.when(owned)
-    def _():
-        past_here().wait()
-
-    stored = past_buf[...].reshape(own * bunches, width)
+    stored = jnp.concatenate(
+        [past_buf[i][:, side * width : (side + 1) * width] for i in range(own) for side in range(2)],
+        axis=0,
+    )
     for copy in loads[5:]:
         copy.wait()
     raw = dot3_t(split(to_raw_in[...]), split(dot3(w_past, split(stored))))
     convolved = jnp.concatenate([raw[:half], raw[half:]], axis=1)
 
-    whole(now_buf, now_send, now_recv).wait_recv()
+    for o in range(1, sections):
+        @pl.when(o <= t)
+        def _():
+            now_copy(o).wait_recv()
+
     gathered = jnp.concatenate(
         [now_buf[i].reshape(half, LANES) for i in range(sections)], axis=1
     )
@@ -336,7 +358,11 @@
         for o in range(1, sections):
             past_copy(o).wait_send()
 
-    whole(now_buf, now_send, now_recv).wait_send()
+    for o in range(1, sections):
+        @pl.when(t + o < sections)
+        def _():
+            now_copy(o).wait_send()
+
     dom_wait.wait_send()
 
     conv_wait = whole(conv_buf, conv_send, conv_recv)
@@ -413,13 +439,17 @@
             pltpu.VMEM((slots // 2, LANES), F32),
             pltpu.VMEM((2, slots // 2, LANES), F32),
             pltpu.VMEM((sections, chunks, 8, LANES), F32),
-            pltpu.VMEM((own, bunches, width), F32),
+            pltpu.VMEM((bunches, width), F32),
+            pltpu.VMEM((bunches // 2, 2 * width), F32),
+            pltpu.VMEM((own, bunches // 2, 2 * width), F32),
             pltpu.VMEM((doms, chunks, 8, LANES), F32),
             pltpu.VMEM((doms, half, LANES), F32),
             dma((10,)),
             dma((sections - 1,)),
             dma((own,)),
-            dma((6,)),
+            dma((sections - 1,)),
+            dma((sections - 1,)),
+            dma((4,)),
         ],
         compiler_params=pltpu.CompilerParams(
             collective_id=0, has_side_effects=True, vmem_limit_bytes=56 * 1024 * 1024

time: 19.8 us -> 17.6 us (0.89)
  the two profiles are of different devices: /device:TPU:0 before, /device:TPU:17 now
where the time goes in v7:
time: 17.6 us; the launch traced here: 17.5 us
  Pallas kernels  15.9 us (90%)
  local copies, waits for them, and re-layouts  0.91 us (5%)
  between operations  0.68 us (4%)
    pallas_call x1, Pallas kernels, local(): pl.pallas_call(functools.partial(moments_kernel, sections, doms, orders),...  14.7 us
    pallas_call x1, Pallas kernels, local(): pl.pallas_call(track_kernel, out_shape=(jax.ShapeDtypeStruct(particles.sh...  1.17 us
    unnamed x6, local copies, waits for them, and re-layouts  0.91 us

profile of v7, /device:TPU:17, one launch (start us, length us, event | category | flops | bytes accessed | tf_op | source)
XLA Modules:
  0.0 17.5 jit_solution(18372155237412120981)
XLA Ops:
  0.6 0.0 copy-start
  0.6 0.0 copy-start.1
  0.7 14.7 %moments.1.table = f32[136,256]{1,0:T(8,128)} custom-call(f32[4,64,1024]{2,1,0:T(8,128)} %particles.3, s32[64,1024]{1,0:T(8,128)} %bins.3, s32[1,64]{1,0:T(1,128)} %bitcast.2, f32[2,64,64]{2,1,0:T(8,128)} %past.1, f32[1535]{0:T(1024)} %lags.1, f32[64,64]{1,0:T(8,128)} %wake.1, f32[1,2]{1,0:T(1,128)} %bitcast.3, f32[64,64]{1,0:T(8,128)} %constant.4.clone.to_moments, ...), custom_call_target="tpu_custom_call" | custom-call | tf_op jit(solution)/shard_map/moments/pallas_call | solution.py:421
  15.4 0.0 copy-done
  15.4 0.0 copy-done.1
  15.4 0.0 copy-start.2
  15.4 0.9 %copy-done.2 = f32[136,256]{1,0:T(8,128)S(1)} copy-done((f32[136,256]{1,0:T(8,128)S(1)}, f32[136,256]{1,0:T(8,128)}, u32[]{:S(2)}) %copy-start.2) | copy-done | bytes 139288
  16.3 1.2 %track.1 = (f32[4,64,1024]{2,1,0:T(8,128)}, f32[64,64]{1,0:T(8,128)}) custom-call(f32[4,64,1024]{2,1,0:T(8,128)S(1)} %copy-done, s32[64,1024]{1,0:T(8,128)S(1)} %copy-done.1, f32[136,256]{1,0:T(8,128)S(1)} %copy-done.2), custom_call_target="tpu_custom_call" | custom-call | tf_op jit(solution)/shard_map/track/pallas_call | solution.py:468
Async XLA Ops:
  0.6 14.7 %copy-start = (f32[4,64,1024]{2,1,0:T(8,128)S(1)}, f32[4,64,1024]{2,1,0:T(8,128)}, u32[]{:S(2)}) copy-start(f32[4,64,1024]{2,1,0:T(8,128)} %particles.3) | copy-start | bytes 3145732
  0.6 14.7 %copy-start.1 = (s32[64,1024]{1,0:T(8,128)S(1)}, s32[64,1024]{1,0:T(8,128)}, u32[]{:S(2)}) copy-start(s32[64,1024]{1,0:T(8,128)} %bins.3) | copy-start | bytes 786436
  15.4 0.9 %copy-start.2 = (f32[136,256]{1,0:T(8,128)S(1)}, f32[136,256]{1,0:T(8,128)}, u32[]{:S(2)}) copy-start(f32[136,256]{1,0:T(8,128)} %moments.1.table) | copy-start | bytes 417796
